TPU v7x, 128 devices: a whole 4x4x4 slice. The times are simulated.
128 devices in a mesh: row: 8 (over z, core), col: 16 (over y, x).
Axes of the slice: x: 4, y: 4, z: 4, core: 2. Of those that a mesh axis runs over, the one named last changes fastest.
Arguments:
- features: float32 [2048, 4, 9, 1920], P(('row', 'col')), may hold values from -12 to 12, as said below
- query_row: int32 [8192], P(('row', 'col')), may hold values from 0 to 15
- target_device: int32 [8192, 1], P(('row', 'col')), may hold values from 0 to 127; in each aligned block of 64 rows (0 to 63, 64 to 127, ...) no two rows name the same one
- target_row: int32 [8192], P(('row', 'col')), may hold values from 0 to 15
- pair_count: int32 [128], P(('row', 'col')), may hold values from 1 to 64, 6144 in all
- conv_first: bfloat16 [9, 32], replicated, may hold values from -2 to 2
- conv_second: bfloat16 [288, 64], replicated, may hold values from -0.5 to 0.5
- conv_third: bfloat16 [576, 128], replicated, may hold values from -0.375 to 0.375
- conv_last: bfloat16 [1152, 1], replicated, may hold values from -0.25 to 0.25
Outputs:
- maps: float32 [8192, 16], P(('row', 'col'))
- scores: float32 [8192], P(('row', 'col'))
Inputs may be any that keep to these rules, and one draw needn't show every extreme that they name: Region features are finite values of order one. `target_device`: among the 64 slots of one device, at most 1 name one target device; this is reached.
All inputs are finite; a program needn't handle non-finite values. No bound on the sum of `pair_count` on one device may be relied on, other than what follows from the above.
Results may differ from a plain program's by a relative error of at most 0.004.
Values may be sent and summed in bfloat16 or wider, within the bound.
A program may use at most 128 MiB of HBM per device.

v0:
```python
import jax
import jax.numpy as jnp
from jax import lax
from jax.sharding import PartitionSpec as P

REGIONS = 9
FRAMES = 4
CAPACITY = 1


def unit_rows(block):
    scale = 1.0 / jnp.sqrt(jnp.sum(block * block, axis=-1, keepdims=True) + 1e-06)
    return (block * scale).astype(jnp.bfloat16)


def convolve(activations, kernel):
    frames = activations.shape[1]
    channels = activations.shape[3]
    padded = jnp.pad(activations, ((0, 0), (1, 1), (1, 1), (0, 0)))
    wide = jnp.concatenate([padded[:, :, shift : shift + frames, :] for shift in range(3)], axis=-1)
    parts = kernel.astype(jnp.float32).reshape(3, 3 * channels, kernel.shape[1])
    total = jnp.zeros((activations.shape[0], frames, frames, kernel.shape[1]), jnp.float32)
    for shift in range(3):
        total = total + jnp.einsum(
            "bijc,co->bijo",
            wide[:, shift : shift + frames],
            parts[shift],
            precision=lax.Precision.HIGHEST,
        )
    return total


def compare_pairs(left, right, kernels):
    batch = left.shape[0]
    similarity = jnp.einsum("bxd,byd->bxy", left, right, preferred_element_type=jnp.float32)
    similarity = similarity.reshape(batch, FRAMES, REGIONS, FRAMES, REGIONS)
    frame_sim = jnp.mean(jnp.max(similarity, axis=4), axis=2)
    hidden = frame_sim[..., None]
    for kernel in kernels[:3]:
        hidden = jax.nn.relu(convolve(hidden, kernel))
    final = convolve(hidden, kernels[3])[..., 0]
    return jnp.clip(final, -1.0, 1.0).reshape(batch, FRAMES * FRAMES)


def compare_blocks(left_table, left_index, right_table, right_index, kernels):
    total_slots = left_index.shape[0]
    block_rows = min(16, total_slots)
    groups = total_slots // block_rows

    def compute_group(indices):
        left_ids, right_ids = indices
        return compare_pairs(left_table[left_ids], right_table[right_ids], kernels)

    refined = lax.map(
        compute_group,
        (left_index.reshape(groups, block_rows), right_index.reshape(groups, block_rows)),
    )
    return refined.reshape(total_slots, FRAMES * FRAMES)


def move_blocks(blocks, labels):
    return (
        lax.all_to_all(blocks, ("row", "col"), split_axis=0, concat_axis=0, tiled=True),
        lax.all_to_all(labels, ("row", "col"), split_axis=0, concat_axis=0, tiled=True),
    )


def per_device(
    features,
    query_row,
    target_device,
    target_row,
    pair_count,
    conv_first,
    conv_second,
    conv_third,
    conv_last,
):
    kernels = (conv_first, conv_second, conv_third, conv_last)
    peers = lax.axis_size(("row", "col"))
    pair_slots = query_row.shape[0]
    buffer_slots = peers * CAPACITY
    table = unit_rows(features.reshape(features.shape[0], FRAMES * REGIONS, features.shape[3]))
    destination = target_device[:, 0]
    positions = jnp.arange(pair_slots, dtype=jnp.int32)
    earlier_same = (destination[:, None] == destination[None, :]) & (
        positions[None, :] < positions[:, None]
    )
    rank_in_peer = jnp.sum(earlier_same.astype(jnp.int32), axis=1)
    slot_index = destination * CAPACITY + rank_in_peer
    is_live = positions < pair_count[0]
    wanted_rows = jnp.where(is_live, target_row, -1)
    empty_marks = jnp.full((buffer_slots,), -1, jnp.int32)
    outgoing = jnp.where(is_live[:, None, None], table[query_row], jnp.zeros((), jnp.bfloat16))
    send_blocks = (
        jnp.zeros((buffer_slots,) + table.shape[1:], jnp.bfloat16).at[slot_index].set(outgoing)
    )
    send_marks = empty_marks.at[slot_index].set(wanted_rows)
    arrived, requested = move_blocks(send_blocks, send_marks)
    slot_order = jnp.arange(buffer_slots, dtype=jnp.int32)
    refined = compare_blocks(arrived, slot_order, table, jnp.maximum(requested, 0), kernels)
    refined = jnp.where((requested >= 0)[:, None], refined, jnp.float32(0.0))
    returned = lax.all_to_all(refined, ("row", "col"), split_axis=0, concat_axis=0, tiled=True)
    maps = returned[slot_index]
    scores = jnp.mean(jnp.max(maps.reshape(pair_slots, FRAMES, FRAMES), axis=2), axis=1)
    return (maps, scores)


def solution(mesh):
    return jax.shard_map(
        per_device,
        mesh=mesh,
        in_specs=(
            P(("row", "col"), None, None, None),
            P(("row", "col")),
            P(("row", "col"), None),
            P(("row", "col")),
            P(("row", "col")),
            P(),
            P(),
            P(),
            P(),
        ),
        out_specs=(P(("row", "col"), None), P(("row", "col"))),
        check_vma=False,
    )
```

profile of v0, /device:TPU:1, one launch (start us, length us, event | category | flops | bytes accessed | tf_op | source)
XLA Modules:
  0.0 591.4 jit_solution(76698914154221315)
XLA Ops:
  5.0 11.5 %all-to-all-start = ((s32[128,1,1]{2,1,0:T(1,128)}), s32[128,1,1]{2,1,0:T(1,128)S(1)}, u32[]{:S(2)}, u32[]{:S(2)}) async-start(s32[128,1,1]{2,1,0:T(1,128)} %copy.62), calls=%async_computation | async-start | bytes 131072 | tf_op jit(solution)/shard_map/all_to_all | solution.py:64
  16.5 4.7 copy.63
  22.6 3.6 fusion.43
  26.2 6.4 %gather_fusion.2 = bf16[64,36,1920]{2,1,0:T(8,128)(2,1)} fusion(bf16[16,36,1920]{2,1,0:T(8,128)(2,1)S(1)} %fusion.43, s32[1024]{0:T(1024)S(1)} %pad_clamp_fusion.3), kind=kCustom, calls=%fused_computation.2 | custom fusion | bytes 17694976 | tf_op jit(solution)/shard_map/gather | solution.py:94
  32.5 8.5 %broadcast_select_fusion = bf16[64,36,1920]{2,1,0:T(8,128)(2,1)} fusion(bf16[64,36,1920]{2,1,0:T(8,128)(2,1)} %gather_fusion.2, pred[64]{0:T(512)(128)(4,1)S(1)} %iota_compare_fusion.1), kind=kLoop, calls=%fused_computation.80 | loop fusion | flops 4423680 | bytes 17694784 | tf_op jit(solution)/shard_map/jit(_where)/select_n | solution.py:94
  41.0 6.8 %broadcast_in_dim.57 = bf16[128,36,1920]{2,1,0:T(8,128)(2,1)} broadcast(bf16[]{:T(256)} %constant.87.clone.1), dimensions={} | broadcast | bytes 17694722 | tf_op jit(solution)/shard_map/broadcast_in_dim | solution.py:96
  47.8 23.9 %scatter_fusion = bf16[128,36,1920]{2,1,0:T(8,128)(2,1)} fusion(bf16[128,36,1920]{2,1,0:T(8,128)(2,1)} %broadcast_in_dim.57, s32[64]{0:T(128)S(1)} %fusion.45, bf16[64,36,1920]{2,1,0:T(8,128)(2,1)} %broadcast_select_fusion), kind=kCustom, calls=%fused_computation.5 | custom fusion | bytes 26542336 | tf_op jit(solution)/shard_map/scatter | solution.py:96
  71.8 10.2 %all-to-all-start.1 = ((bf16[128,36,1920]{2,1,0:T(8,128)(2,1)}), bf16[128,36,1920]{2,1,0:T(8,128)(2,1)}, u32[]{:S(2)}, u32[]{:S(2)}) async-start(bf16[128,36,1920]{2,1,0:T(8,128)(2,1)} %scatter_fusion), calls=%async_computation.1 | async-start | bytes 39321600 | tf_op jit(solution)/shard_map/all_to_all | solution.py:63
  82.0 2.4 maximum_reduce_fusion
  84.4 2.4 compare_reduce_fusion
  86.8 275.8 %all-to-all-done.1 = bf16[128,36,1920]{2,1,0:T(8,128)(2,1)} async-done(((bf16[128,36,1920]{2,1,0:T(8,128)(2,1)}), bf16[128,36,1920]{2,1,0:T(8,128)(2,1)}, u32[]{:S(2)}, u32[]{:S(2)}) %all-to-all-start.1) | async-done | bytes 17694752 | tf_op jit(solution)/shard_map/all_to_all | solution.py:63
  362.6 186.3 %while.12 = (s32[]{:T(128)}, f32[8,16,16]{2,1,0:T(8,128)S(1)}, s32[8,16]{1,0:T(8,128)S(1)}, bf16[128,36,1920]{2,1,0:T(8,128)(2,1)}, s32[8,16]{1,0:T(8,128)S(1)},...) while((s32[]{:T(128)}, f32[8,16,16]{2,1,0:T(8,128)S(1)}, ...), condition=%wide.region_7.8_spmd, body=%wide.region_4.7_spmd.sunk | while | flops 368768864 | bytes 39001796 | solution.py:54
  362.7 1.4 copy-done
  364.1 7.5 %gather_fusion = bf16[16,36,1920]{2,1,0:T(8,128)(2,1)S(1)} fusion(bf16[128,36,1920]{2,1,0:T(8,128)(2,1)} %get-tuple-element.306, s32[1024]{0:T(1024)S(1)} %pad_clamp_fusion.6), kind=kCustom, calls=%fused_computation.clone.1 | custom fusion | bytes 4423744 | tf_op jit(solution)/shard_map/while/body/eval_jaxpr/gather | solution.py:52
  371.6 4.0 gather_fusion.1
  375.6 2.5 fusion.100
  382.7 1.0 fusion.109
  383.8 1.0 fusion.108
  384.8 1.0 fusion.107
  386.0 1.4 copy-done
  387.4 7.5 %gather_fusion = bf16[16,36,1920]{2,1,0:T(8,128)(2,1)S(1)} fusion(bf16[128,36,1920]{2,1,0:T(8,128)(2,1)} %get-tuple-element.306, s32[1024]{0:T(1024)S(1)} %pad_clamp_fusion.6), kind=kCustom, calls=%fused_computation.clone.1 | custom fusion | bytes 4423744 | tf_op jit(solution)/shard_map/while/body/eval_jaxpr/gather | solution.py:52
  394.9 4.0 gather_fusion.1
  398.9 2.5 fusion.100
  407.0 1.0 fusion.108
  408.1 1.0 fusion.107
  409.2 1.4 copy-done
  410.7 7.5 %gather_fusion = bf16[16,36,1920]{2,1,0:T(8,128)(2,1)S(1)} fusion(bf16[128,36,1920]{2,1,0:T(8,128)(2,1)} %get-tuple-element.306, s32[1024]{0:T(1024)S(1)} %pad_clamp_fusion.6), kind=kCustom, calls=%fused_computation.clone.1 | custom fusion | bytes 4423744 | tf_op jit(solution)/shard_map/while/body/eval_jaxpr/gather | solution.py:52
  418.2 4.0 gather_fusion.1
  422.2 2.5 fusion.100
  430.3 1.0 fusion.108
  431.4 1.0 fusion.107
  432.5 1.4 copy-done
  434.0 7.5 %gather_fusion = bf16[16,36,1920]{2,1,0:T(8,128)(2,1)S(1)} fusion(bf16[128,36,1920]{2,1,0:T(8,128)(2,1)} %get-tuple-element.306, s32[1024]{0:T(1024)S(1)} %pad_clamp_fusion.6), kind=kCustom, calls=%fused_computation.clone.1 | custom fusion | bytes 4423744 | tf_op jit(solution)/shard_map/while/body/eval_jaxpr/gather | solution.py:52
  441.5 4.0 gather_fusion.1
  445.5 2.5 fusion.100
  453.6 1.0 fusion.108
  454.6 1.0 fusion.107
  455.8 1.4 copy-done
  457.2 7.5 %gather_fusion = bf16[16,36,1920]{2,1,0:T(8,128)(2,1)S(1)} fusion(bf16[128,36,1920]{2,1,0:T(8,128)(2,1)} %get-tuple-element.306, s32[1024]{0:T(1024)S(1)} %pad_clamp_fusion.6), kind=kCustom, calls=%fused_computation.clone.1 | custom fusion | bytes 4423744 | tf_op jit(solution)/shard_map/while/body/eval_jaxpr/gather | solution.py:52
  464.8 4.0 gather_fusion.1
  468.8 2.5 fusion.100
  476.9 1.0 fusion.108
  477.9 1.0 fusion.107
  479.1 1.4 copy-done
  480.5 7.5 %gather_fusion = bf16[16,36,1920]{2,1,0:T(8,128)(2,1)S(1)} fusion(bf16[128,36,1920]{2,1,0:T(8,128)(2,1)} %get-tuple-element.306, s32[1024]{0:T(1024)S(1)} %pad_clamp_fusion.6), kind=kCustom, calls=%fused_computation.clone.1 | custom fusion | bytes 4423744 | tf_op jit(solution)/shard_map/while/body/eval_jaxpr/gather | solution.py:52
  488.1 4.0 gather_fusion.1
  492.0 2.5 fusion.100
  500.2 1.0 fusion.108
  501.2 1.0 fusion.107
  502.4 1.4 copy-done
  503.8 7.5 %gather_fusion = bf16[16,36,1920]{2,1,0:T(8,128)(2,1)S(1)} fusion(bf16[128,36,1920]{2,1,0:T(8,128)(2,1)} %get-tuple-element.306, s32[1024]{0:T(1024)S(1)} %pad_clamp_fusion.6), kind=kCustom, calls=%fused_computation.clone.1 | custom fusion | bytes 4423744 | tf_op jit(solution)/shard_map/while/body/eval_jaxpr/gather | solution.py:52
  511.3 4.0 gather_fusion.1
  515.3 2.5 fusion.100
  523.5 1.0 fusion.108
  524.5 1.0 fusion.107
  525.7 1.4 copy-done
  527.1 7.5 %gather_fusion = bf16[16,36,1920]{2,1,0:T(8,128)(2,1)S(1)} fusion(bf16[128,36,1920]{2,1,0:T(8,128)(2,1)} %get-tuple-element.306, s32[1024]{0:T(1024)S(1)} %pad_clamp_fusion.6), kind=kCustom, calls=%fused_computation.clone.1 | custom fusion | bytes 4423744 | tf_op jit(solution)/shard_map/while/body/eval_jaxpr/gather | solution.py:52
  534.6 4.0 gather_fusion.1
  538.6 2.5 fusion.100
  545.7 1.0 fusion.109
  546.7 1.0 fusion.108
  547.8 1.0 fusion.107
  549.7 30.8 %all-to-all-start.2 = ((f32[128,1,16]{2,1,0:T(1,128)}), f32[128,1,16]{2,1,0:T(1,128)S(1)}, u32[]{:S(2)}, u32[]{:S(2)}) async-start(f32[128,1,16]{2,1,0:T(1,128)} %broadcast_select_fusion.1), calls=%async_computation.2 | async-start | bytes 131072 | tf_op jit(solution)/shard_map/all_to_all | solution.py:103
  580.5 9.6 %all-to-all-done.2 = f32[128,1,16]{2,1,0:T(1,128)S(1)} async-done(((f32[128,1,16]{2,1,0:T(1,128)}), f32[128,1,16]{2,1,0:T(1,128)S(1)}, u32[]{:S(2)}, u32[]{:S(2)}) %all-to-all-start.2) | async-done | bytes 8224 | tf_op jit(solution)/shard_map/all_to_all | solution.py:103
  (278 shorter events, 49.9 us)
Async XLA Ops:
  5.0 16.3 %slice-start = ((s8[4423680]{0:T(1024)(128)(4,1)}), s8[229376]{0:T(1024)(128)(4,1)S(1)}, s32[]{:S(2)}) async-start(s8[4423680]{0:T(1024)(128)(4,1)} %bitcast.154), calls=%async_computation.3 | async-start | bytes 458752
  5.0 66.7 %all-to-all-start = ((s32[128,1,1]{2,1,0:T(1,128)}), s32[128,1,1]{2,1,0:T(1,128)S(1)}, u32[]{:S(2)}, u32[]{:S(2)}) async-start(s32[128,1,1]{2,1,0:T(1,128)} %copy.62), calls=%async_computation | async-start | bytes 131072 | tf_op jit(solution)/shard_map/all_to_all | solution.py:64
  16.5 4.8 slice-start.1
  21.3 1.3 copy-start.7
  71.7 290.9 %copy-start.2 = (bf16[576,128]{1,0:T(8,128)(2,1)S(1)}, bf16[576,128]{1,0:T(8,128)(2,1)}, u32[]{:S(2)}) copy-start(bf16[576,128]{1,0:T(8,128)(2,1)} %param.18) | copy-start | bytes 442372
  71.7 290.9 %copy-start.3 = (bf16[288,64]{0,1:T(8,128)(2,1)S(1)}, bf16[288,64]{0,1:T(8,128)(2,1)}, u32[]{:S(2)}) copy-start(bf16[288,64]{0,1:T(8,128)(2,1)} %param.17) | copy-start | bytes 110596
  71.7 290.9 %copy-start.4 = (bf16[9,32]{1,0:T(8,128)(2,1)S(1)}, bf16[9,32]{1,0:T(8,128)(2,1)}, u32[]{:S(2)}) copy-start(bf16[9,32]{1,0:T(8,128)(2,1)} %param.16) | copy-start | bytes 1732
  71.7 290.9 %copy-start.6 = (bf16[1152,1]{0,1:T(2,128)(2,1)S(1)}, bf16[1152,1]{0,1:T(2,128)(2,1)}, u32[]{:S(2)}) copy-start(bf16[1152,1]{0,1:T(2,128)(2,1)} %param.19) | copy-start | bytes 6916
  71.8 290.9 %all-to-all-start.1 = ((bf16[128,36,1920]{2,1,0:T(8,128)(2,1)}), bf16[128,36,1920]{2,1,0:T(8,128)(2,1)}, u32[]{:S(2)}, u32[]{:S(2)}) async-start(bf16[128,36,1920]{2,1,0:T(8,128)(2,1)} %scatter_fusion), calls=%async_computation.1 | async-start | bytes 39321600 | tf_op jit(solution)/shard_map/all_to_all | solution.py:63
  362.6 1.5 copy-start
  380.3 5.7 copy-start.1
  385.9 1.5 copy-start
  403.5 5.7 copy-start.1
  409.2 1.5 copy-start
  426.8 5.7 copy-start.1
  432.5 1.5 copy-start
  450.1 5.7 copy-start.1
  455.8 1.5 copy-start
  473.4 5.7 copy-start.1
  479.1 1.5 copy-start
  496.7 5.7 copy-start.1
  502.4 1.5 copy-start
  520.0 5.7 copy-start.1
  525.6 1.5 copy-start
  543.3 5.7 copy-start.1
  549.7 40.4 %all-to-all-start.2 = ((f32[128,1,16]{2,1,0:T(1,128)}), f32[128,1,16]{2,1,0:T(1,128)S(1)}, u32[]{:S(2)}, u32[]{:S(2)}) async-start(f32[128,1,16]{2,1,0:T(1,128)} %broadcast_select_fusion.1), calls=%async_computation.2 | async-start | bytes 131072 | tf_op jit(solution)/shard_map/all_to_all | solution.py:103
  590.8 0.6 copy-start.5
where the time goes:
time: 593 us; the launch traced here: 591 us
  waiting for transfers between devices  285 us (48%)
  local copies, waits for them, and re-layouts  155 us (26%)
  matrix products  66.8 us (11%)
  starting transfers between devices  52.4 us (9%)
  other arithmetic  28.7 us (5%)
    all_to_all x1, waiting for transfers between devices, move_blocks(): lax.all_to_all(blocks, ('row', 'col'), split_axis=0, concat_axis=0, tiled...  276 us
    gather x16, local copies, waits for them, and re-layouts, compute_group(): return compare_pairs(left_table[left_ids], right_table[right_ids], kernels)  92 us
    dot_general x96, matrix products, convolve(): jnp.einsum('bijc,co->bijo', wide[:, shift:shift + frames], parts[shift],...  46.7 us
    all_to_all x1, starting transfers between devices, per_device(): lax.all_to_all(refined, ('row', 'col'), split_axis=0, concat_axis=0, tile...  30.8 us
    scatter x1, local copies, waits for them, and re-layouts, per_device(): jnp.zeros((buffer_slots,) + table.shape[1:], jnp.bfloat16).at[slot_index]  23.9 us
    dot_general x8, matrix products, compare_pairs(): jnp.einsum('bxd,byd->bxy', left, right, preferred_element_type=jnp.float32)  20.1 us
    while x40, local copies, waits for them, and re-layouts  12.2 us
  transfers between devices with their start and end apart: 3, of which 2 were waited for; matrix products, arithmetic and copies ran while one was open for 10% of the time, Pallas kernels for 0%

commit v1 on v0

v1 whole, which is shorter than its diff:
```python
import functools

import jax
import jax.numpy as jnp
from jax import lax
from jax.experimental import pallas as pl
from jax.experimental.pallas import tpu as pltpu
from jax.sharding import PartitionSpec as P

MESH = pl.DeviceIdType.MESH
CLIPS = 16
FRAMES = 4
REGIONS = 9
DIM = 1920
LANES = 128
SLICES = DIM // LANES
COLS = 16
ROWS = 8
MAIN = 32
TAILS = CLIPS * MAIN
BLOCK = CLIPS * FRAMES * REGIONS
SLOTS = 64
HALVES = 22
GROUPS = HALVES // 2
GROUP_ROWS = 2 * 40
PAY = GROUPS * GROUP_ROWS
VMEM_LIMIT = 60 * 2**20


def gather_kernel(
    feat, idx, table, idx_all, units, scales, a_send, a_recv, i_send, i_recv, b_send, b_recv, own_sem
):
    row = lax.axis_index("row")
    me = lax.axis_index("col")
    z = row // 2
    core = lax.rem(row, 2)
    rows_z = lambda step: lax.rem(z + step, 4) * 2 + core
    rows_mate = lambda step: lax.rem(z + step, 4) * 2 + 1 - core
    mate = z * 2 + 1 - core

    barrier = pltpu.get_barrier_semaphore()

    def greet(i, carry):
        pl.semaphore_signal(
            barrier, inc=1, device_id=(row, lax.rem(me + i, COLS)), device_id_type=MESH
        )
        return carry

    lax.fori_loop(1, COLS, greet, 0)
    for other in (rows_z(1), rows_z(2), rows_z(3), mate):
        pl.semaphore_signal(barrier, inc=1, device_id=(other, me), device_id_type=MESH)

    def measure(i, carry):
        c = i // FRAMES
        f = lax.rem(i, FRAMES)
        x = feat[c, f]
        total = jnp.sum(x * x, axis=-1, keepdims=True)
        scales[c, f] = jnp.broadcast_to(1.0 / jnp.sqrt(total + 1e-06), (REGIONS, LANES))
        return carry

    lax.fori_loop(0, CLIPS * FRAMES, measure, 0)
    pl.semaphore_wait(barrier, COLS - 1 + 4)

    def idx_copy(i):
        return pltpu.make_async_remote_copy(
            src_ref=idx,
            dst_ref=idx_all.at[me],
            send_sem=i_send.at[i],
            recv_sem=i_recv.at[i],
            device_id=(row, lax.rem(me + i, COLS)),
            device_id_type=MESH,
        )

    def slice_copy(i):
        n = lax.rem(me + i, COLS)
        return pltpu.make_async_remote_copy(
            src_ref=units.at[n],
            dst_ref=table.at[row, me],
            send_sem=a_send.at[i],
            recv_sem=a_recv.at[i],
            device_id=(row, n),
            device_id_type=MESH,
        )

    def arrival(i, s):
        return pltpu.make_async_remote_copy(
            src_ref=units.at[0],
            dst_ref=table.at[row, s],
            send_sem=a_send.at[i],
            recv_sem=a_recv.at[i],
            device_id=(row, s),
            device_id_type=MESH,
        )

    def fill(n):
        lanes = pl.ds(pl.multiple_of(n * LANES, LANES), LANES)

        def quad(j, carry):
            tails = []
            for k in range(4):
                c = j * 4 + k
                parts = [feat[c, f, :, lanes] * scales[c, f] for f in range(FRAMES)]
                main = jnp.concatenate([p[:8] for p in parts], axis=0)
                units[n, pl.ds(pl.multiple_of(c * MAIN, MAIN), MAIN), :] = main.astype(jnp.bfloat16)
                tails += [p[8:9] for p in parts]
            tail = jnp.concatenate(tails, axis=0)
            units[n, pl.ds(pl.multiple_of(TAILS + j * 16, 16), 16), :] = tail.astype(jnp.bfloat16)
            return carry

        lax.fori_loop(0, CLIPS // 4, quad, 0)

    own_idx = pltpu.make_async_copy(idx, idx_all.at[me], own_sem.at[1])
    own_idx.start()

    def send_idx(i, carry):
        idx_copy(i).start()
        return carry

    lax.fori_loop(1, COLS, send_idx, 0)

    own = pltpu.make_async_copy(units.at[me], table.at[row, me], own_sem.at[0])

    @pl.when(me < SLICES)
    def _():
        fill(me)
        own.start()

    def send_slice(i, carry):
        n = lax.rem(me + i, COLS)

        @pl.when(n < SLICES)
        def _():
            fill(n)
            slice_copy(i).start()

        return carry

    lax.fori_loop(1, COLS, send_slice, 0)

    def forward(source_row, s, target_row, kind, j):
        return pltpu.make_async_remote_copy(
            src_ref=table.at[source_row, s],
            dst_ref=table.at[source_row, s],
            send_sem=b_send.at[kind, j],
            recv_sem=b_recv.at[kind, j],
            device_id=(target_row, me),
            device_id_type=MESH,
        )

    @pl.when(me < SLICES)
    def _():
        own.wait()

        def spread(j, carry):
            s = lax.rem(me - j + COLS, COLS)

            @pl.when(j > 0)
            def _():
                arrival(j, s).wait_recv()

            for step in (1, 3, 2):
                forward(row, s, rows_z(step), step, j).start()
            forward(row, s, mate, 4, j).start()
            return carry

        lax.fori_loop(0, COLS, spread, 0)

        def relay(j, carry):
            s = lax.rem(me - j + COLS, COLS)
            for step in (1, 3, 2):
                forward(rows_z(4 - step), s, rows_z(step), step, j).wait_recv()
                forward(rows_z(4 - step), s, mate, 4 + step, j).start()
            return carry

        lax.fori_loop(0, COLS, relay, 0)

        def finish(j, carry):
            s = lax.rem(me - j + COLS, COLS)
            forward(rows_mate(0), s, mate, 4, j).wait_recv()
            forward(row, s, mate, 4, j).wait_send()
            for step in (1, 3, 2):
                forward(rows_mate(4 - step), s, mate, 4 + step, j).wait_recv()
                forward(rows_z(4 - step), s, mate, 4 + step, j).wait_send()
                forward(row, s, rows_z(step), step, j).wait_send()
            return carry

        lax.fori_loop(0, COLS, finish, 0)

    own_idx.wait()

    def drain(i, carry):
        idx_copy(i).wait()

        @pl.when(lax.rem(me + i, COLS) < SLICES)
        def _():
            slice_copy(i).wait_send()

        return carry

    lax.fori_loop(1, COLS, drain, 0)


def gather(features, packed):
    dma = pltpu.SemaphoreType.DMA
    return pl.pallas_call(
        gather_kernel,
        out_shape=(
            jax.ShapeDtypeStruct((ROWS, COLS, BLOCK, LANES), jnp.bfloat16),
            jax.ShapeDtypeStruct((COLS, 8, LANES), jnp.int32),
        ),
        in_specs=[pl.BlockSpec(memory_space=pltpu.VMEM)] * 2,
        out_specs=[pl.BlockSpec(memory_space=pl.ANY)] * 2,
        scratch_shapes=[
            pltpu.VMEM((SLICES, BLOCK, LANES), jnp.bfloat16),
            pltpu.VMEM((CLIPS, FRAMES, REGIONS, LANES), jnp.float32),
            dma((COLS,)),
            dma((COLS,)),
            dma((COLS,)),
            dma((COLS,)),
            dma((8, COLS)),
            dma((8, COLS)),
            dma((2,)),
        ],
        compiler_params=pltpu.CompilerParams(
            collective_id=0, has_side_effects=True, vmem_limit_bytes=VMEM_LIMIT
        ),
    )(features, packed)


def compare_kernel(idx, table, pay, tails, products):
    row = lax.axis_index("row")
    me = lax.axis_index("col")

    @pl.when(me < SLICES)
    def _():
        def widen(i, carry):
            r = i // COLS
            s = lax.rem(i, COLS)
            tails[pl.ds(pl.multiple_of(i * 64, 64), 64), :] = table[
                r, s, TAILS : TAILS + 64, :
            ].astype(jnp.float32)
            return carry

        lax.fori_loop(0, ROWS * COLS, widen, 0)
        sub = lax.broadcasted_iota(jnp.int32, (8, LANES), 0)
        lane = lax.broadcasted_iota(jnp.int32, (8, LANES), 1)
        block = lax.rem(lane // MAIN, 4)
        third = lax.rem(lane, 8)
        choice = jnp.where(block < 3, block, third)

        def pick(parts):
            return jnp.where(choice == 0, parts[0], jnp.where(choice == 1, parts[1], parts[2]))

        def group(i, carry):
            n = i // GROUPS
            g = lax.rem(i, GROUPS)
            halves = []
            queries = []
            for b in range(2):
                main = []
                rows = []
                asked = []
                for t in range(3):
                    slot = jnp.minimum(t * HALVES + g * 2 + b, SLOTS - 1)
                    word = idx[n, 0, slot]
                    asked.append(word & 15)
                    clip = (word >> 4) & 15
                    device = word >> 8
                    start = pl.multiple_of(clip * MAIN, MAIN)
                    main.append(table[device >> 4, device & 15, pl.ds(start, MAIN), :])
                    rows.append((device * CLIPS + clip) * FRAMES)
                tail = []
                for f in range(FRAMES):
                    got = [
                        jnp.broadcast_to(tails[pl.ds(rows[t] + f, 1), :], (8, LANES))
                        for t in range(3)
                    ]
                    tail.append(jnp.where(sub == 0, got[0], jnp.where(sub == 1, got[1], got[2])))
                halves += main + [jnp.concatenate(tail, axis=0).astype(jnp.bfloat16)]
                queries.append(asked)
            targets = jnp.concatenate(halves, axis=0)
            products[...] = lax.dot_general(
                table[row, n],
                targets,
                (((1,), (1,)), ((), ())),
                preferred_element_type=jnp.float32,
            )
            ends = []
            for b in range(2):
                cols = slice(b * LANES, (b + 1) * LANES)
                for f in range(FRAMES):
                    parts = [
                        products[pl.ds(pl.multiple_of(q * MAIN + f * 8, 8), 8), cols]
                        for q in queries[b]
                    ]
                    ends.append((b, f, pick(parts)))
            base = pl.multiple_of(g * GROUP_ROWS, 16)
            for b in range(2):
                kept = [v for bb, f, v in ends if bb == b]
                pay[n, pl.ds(base + b * MAIN, MAIN), :] = jnp.concatenate(kept, axis=0).astype(
                    jnp.bfloat16
                )
            last = []
            for b in range(2):
                cols = slice(b * LANES, (b + 1) * LANES)
                parts = []
                for q in queries[b]:
                    pair = products[pl.ds(pl.multiple_of(TAILS + (q >> 1) * 8, 8), 8), cols]
                    parts.append(jnp.where((q & 1) == 0, pair, pltpu.roll(pair, 4, 0)))
                last.append(pick(parts))
            pay[n, pl.ds(base + 2 * MAIN, 16), :] = jnp.concatenate(last, axis=0).astype(
                jnp.bfloat16
            )
            return carry

        lax.fori_loop(0, COLS * GROUPS, group, 0)


def compare(idx_all, table):
    return pl.pallas_call(
        compare_kernel,
        out_shape=jax.ShapeDtypeStruct((COLS, PAY, LANES), jnp.bfloat16),
        in_specs=[
            pl.BlockSpec(memory_space=pltpu.SMEM),
            pl.BlockSpec(memory_space=pltpu.VMEM),
        ],
        out_specs=pl.BlockSpec(memory_space=pltpu.VMEM),
        scratch_shapes=[
            pltpu.VMEM((ROWS * COLS * CLIPS * FRAMES, LANES), jnp.float32),
            pltpu.VMEM((BLOCK, 2 * LANES), jnp.float32),
        ],
        compiler_params=pltpu.CompilerParams(vmem_limit_bytes=VMEM_LIMIT),
    )(idx_all, table)


def return_kernel(pay, got, send, recv, own_sem):
    row = lax.axis_index("row")
    me = lax.axis_index("col")
    barrier = pltpu.get_barrier_semaphore()

    def greet(i, carry):
        pl.semaphore_signal(
            barrier, inc=1, device_id=(row, lax.rem(me + i, COLS)), device_id_type=MESH
        )
        return carry

    lax.fori_loop(1, COLS, greet, 0)
    pl.semaphore_wait(barrier, COLS - 1)

    def copy(i):
        n = lax.rem(me + i, COLS)
        return pltpu.make_async_remote_copy(
            src_ref=pay.at[n],
            dst_ref=got.at[me],
            send_sem=send.at[i],
            recv_sem=recv.at[i],
            device_id=(row, n),
            device_id_type=MESH,
        )

    own = pltpu.make_async_copy(pay.at[me], got.at[me], own_sem)

    @pl.when(me < SLICES)
    def _():
        own.start()

        def start(i, carry):
            copy(i).start()
            return carry

        lax.fori_loop(1, COLS, start, 0)

    def arrive(i, carry):
        @pl.when(lax.rem(me - i + COLS, COLS) < SLICES)
        def _():
            copy(i).wait_recv()

        return carry

    lax.fori_loop(1, COLS, arrive, 0)

    @pl.when(me < SLICES)
    def _():
        own.wait()

        def drain(i, carry):
            copy(i).wait_send()
            return carry

        lax.fori_loop(1, COLS, drain, 0)


def return_pay(pay):
    dma = pltpu.SemaphoreType.DMA
    return pl.pallas_call(
        return_kernel,
        out_shape=jax.ShapeDtypeStruct(pay.shape, pay.dtype),
        in_specs=[pl.BlockSpec(memory_space=pl.ANY)],
        out_specs=pl.BlockSpec(memory_space=pl.ANY),
        scratch_shapes=[dma((COLS,)), dma((COLS,)), dma],
        compiler_params=pltpu.CompilerParams(collective_id=1, has_side_effects=True),
    )(pay)


def split(x):
    high = x.astype(jnp.bfloat16)
    return high, (x - high.astype(jnp.float32)).astype(jnp.bfloat16)


def dot_split(x, kernel):
    high, low = split(x)
    return jnp.dot(high, kernel, preferred_element_type=jnp.float32) + jnp.dot(
        low, kernel, preferred_element_type=jnp.float32
    )


def convolve(padded, kernel):
    channels = padded.shape[3]
    rows = padded.shape[2]
    total = None
    for dy in range(3):
        wide = jnp.concatenate(
            [padded[dy : dy + 4, dx : dx + 4] for dx in range(3)], axis=-1
        ).reshape(16 * rows, 3 * channels)
        part = dot_split(wide, kernel[dy * 3 * channels : (dy + 1) * 3 * channels, :])
        total = part if total is None else total + part
    return total


def finish_kernel(count, got, first, second, third, last, maps, scores, frames, one, two):
    lane = lax.broadcasted_iota(jnp.int32, (8, LANES), 1)
    shift = lambda x, by: pltpu.roll(x, (LANES - by) % LANES, 1)
    frames[...] = jnp.zeros_like(frames)

    def best(x):
        top = jnp.maximum(x, shift(x, 1))
        top = jnp.maximum(top, shift(top, 2))
        top = jnp.maximum(top, shift(top, 4))
        ends = [shift(x, 96 + t - 32 * t) for t in range(3)]
        end = jnp.where(lane < 32, ends[0], jnp.where(lane < 64, ends[1], ends[2]))
        return jnp.maximum(top, end)

    def group(g, carry):
        base = pl.multiple_of(g * GROUP_ROWS, 16)
        total = jnp.zeros((GROUP_ROWS, LANES), jnp.float32)
        for m in range(SLICES):
            total += got[m, pl.ds(base, GROUP_ROWS), :].astype(jnp.float32)
        for b in range(2):
            tail = best(total[2 * MAIN + b * 8 : 2 * MAIN + b * 8 + 8])
            for f in range(FRAMES):
                start = b * MAIN + f * 8
                main = jnp.sum(best(total[start : start + 8]), axis=0, keepdims=True)
                frames[f, pl.ds(g * 2 + b, 1), :] = (main + tail[f : f + 1]) * (1.0 / REGIONS)
        return carry

    lax.fori_loop(0, GROUPS, group, 0)

    pairs = 72
    one[...] = jnp.zeros_like(one)
    two[...] = jnp.zeros_like(two)
    ch1 = first.shape[1]
    ch2 = second.shape[1]
    ch3 = third.shape[1]
    taps = first[...].astype(jnp.float32)
    spread = []
    for i in range(FRAMES):
        value = frames[i]
        for j in range(FRAMES):
            spread.append(
                jnp.concatenate(
                    [
                        jnp.broadcast_to(
                            value[:, 32 * t + 8 * j : 32 * t + 8 * j + 1], (24, ch1)
                        )
                        for t in range(3)
                    ],
                    axis=0,
                )
            )
    around = lambda i, j: [
        (dy * 3 + dx, (i + dy - 1) * 4 + j + dx - 1)
        for dy in range(3)
        for dx in range(3)
        if 0 <= i + dy - 1 < 4 and 0 <= j + dx - 1 < 4
    ]
    for i in range(FRAMES):
        for j in range(FRAMES):
            total = jnp.zeros((pairs, ch1), jnp.float32)
            for tap, pos in around(i, j):
                total += spread[pos] * taps[tap : tap + 1, :]
            one[1 + i, 1 + j] = jnp.maximum(total, 0.0)
    hidden = jnp.maximum(convolve(one, second), 0.0)
    two[1:5, 1:5] = hidden.reshape(4, 4, pairs, ch2)
    hidden = jnp.maximum(convolve(two, third), 0.0)
    high, low = split(hidden)
    nt = (((1,), (1,)), ((), ()))
    response = lax.dot_general(
        high, last[...], nt, preferred_element_type=jnp.float32
    ) + lax.dot_general(low, last[...], nt, preferred_element_type=jnp.float32)
    response = response.reshape(16, pairs, response.shape[1])
    tap_lane = lax.broadcasted_iota(jnp.int32, (pairs, response.shape[2]), 1)
    out_lane = lax.broadcasted_iota(jnp.int32, (pairs, LANES), 1)
    result = jnp.zeros((pairs, LANES), jnp.float32)
    for i in range(FRAMES):
        for j in range(FRAMES):
            total = jnp.zeros((pairs, response.shape[2]), jnp.float32)
            for tap, pos in around(i, j):
                total += jnp.where(tap_lane == tap, response[pos], 0.0)
            value = jnp.sum(total, axis=1, keepdims=True)
            result = jnp.where(out_lane == i * 4 + j, value, result)
    line = lax.broadcasted_iota(jnp.int32, (pairs, LANES), 0)
    slot = (line // 24) * HALVES + lax.rem(line, 24)
    result = jnp.where(slot < count[0], jnp.clip(result, -1.0, 1.0), 0.0)
    top = jnp.maximum(result, shift(result, 1))
    top = jnp.maximum(top, shift(top, 2))
    kept = (out_lane < 16) & (lax.rem(out_lane, 4) == 0)
    score = jnp.sum(jnp.where(kept, top, 0.0), axis=1, keepdims=True) * (1.0 / FRAMES)
    for t in range(3):
        amount = min(HALVES, SLOTS - t * HALVES)
        maps[t * HALVES : t * HALVES + amount, :] = result[t * 24 : t * 24 + amount, :16]
        scores[t * HALVES : t * HALVES + amount, :] = score[t * 24 : t * 24 + amount]


def finish(count, got, first, second, third, last):
    vmem = pl.BlockSpec(memory_space=pltpu.VMEM)
    return pl.pallas_call(
        finish_kernel,
        out_shape=(
            jax.ShapeDtypeStruct((SLOTS, FRAMES * FRAMES), jnp.float32),
            jax.ShapeDtypeStruct((SLOTS, 1), jnp.float32),
        ),
        in_specs=[pl.BlockSpec(memory_space=pltpu.SMEM)] + [vmem] * 5,
        out_specs=[vmem] * 2,
        scratch_shapes=[
            pltpu.VMEM((FRAMES, 24, LANES), jnp.float32),
            pltpu.VMEM((6, 6, 72, first.shape[1]), jnp.float32),
            pltpu.VMEM((6, 6, 72, second.shape[1]), jnp.float32),
        ],
        compiler_params=pltpu.CompilerParams(vmem_limit_bytes=VMEM_LIMIT),
    )(count, got, first, second, third, last)


def per_device(
    features,
    query_row,
    target_device,
    target_row,
    pair_count,
    conv_first,
    conv_second,
    conv_third,
    conv_last,
):
    packed = query_row + (target_row << 4) + (target_device[:, 0] << 8)
    packed = jnp.broadcast_to(jnp.pad(packed, (0, LANES - SLOTS))[None], (8, LANES))
    table, idx_all = gather(features, packed)
    pay = compare(idx_all, table)
    got = return_pay(pay)
    last = conv_last.reshape(9, conv_third.shape[1])
    maps, scores = finish(pair_count, got, conv_first, conv_second, conv_third, last)
    return maps, scores[:, 0]


def solution(mesh):
    return jax.shard_map(
        per_device,
        mesh=mesh,
        in_specs=(
            P(("row", "col"), None, None, None),
            P(("row", "col")),
            P(("row", "col"), None),
            P(("row", "col")),
            P(("row", "col")),
            P(),
            P(),
            P(),
            P(),
        ),
        out_specs=(P(("row", "col"), None), P(("row", "col"))),
        check_vma=False,
    )
```

time: 593 us -> 279 us (0.47)
  waiting for transfers between devices: 285 us -> 0 us
  Pallas kernels: 0 us -> 264 us
  local copies, waits for them, and re-layouts: 155 us -> 9.01 us
  matrix products: 66.8 us -> 0 us
  starting transfers between devices: 52.4 us -> 0 us
  other arithmetic: 28.7 us -> 2.01 us
    all_to_all x3 -> x0, waiting for transfers between devices: 285 us -> none  [the longest x1 276 us: move_blocks(): lax.all_to_all(blocks, ('row', 'col'), split_axis=0, concat_axis=0, tiled...]
    pallas_call x0 -> x4, Pallas kernels: none -> 264 us  [the longest x1 132 us: gather(): pl.pallas_call(gather_kernel, out_shape=(jax.ShapeDtypeStruct((ROWS, COLS...]
    gather x18 -> x0, local copies, waits for them, and re-layouts: 98.9 us -> none  [the longest x16 92 us: compute_group(): return compare_pairs(left_table[left_ids], right_table[right_ids], kernels)]
    dot_general x104 -> x0, matrix products: 66.8 us -> none  [the longest x96 46.7 us: convolve(): jnp.einsum('bijc,co->bijo', wide[:, shift:shift + frames], parts[shift],...]
    all_to_all x3 -> x0, starting transfers between devices: 52.4 us -> none  [the longest x1 30.8 us: per_device(): lax.all_to_all(refined, ('row', 'col'), split_axis=0, concat_axis=0, tile...]
    scatter x2 -> x0, local copies, waits for them, and re-layouts: 24.7 us -> none  [the longest x1 23.9 us: per_device(): jnp.zeros((buffer_slots,) + table.shape[1:], jnp.bfloat16).at[slot_index]]
    while x40 -> x0, local copies, waits for them, and re-layouts: 12.2 us -> none
    select_n x13 -> x0, other arithmetic: 10.7 us -> none  [the longest x1 8.49 us: per_device(): jnp.where(is_live[:, None, None], table[query_row], jnp.zeros((), jnp.bfl...]
  transfers between devices with their start and end apart: 3 -> 0, of which waited for: 2 -> 0; matrix products, arithmetic and copies ran while one was open for 10% -> 0% of each run, Pallas kernels for 0% -> 0%
where the time goes in v1:
time: 279 us; the launch traced here: 277 us
  Pallas kernels  264 us (95%)
  local copies, waits for them, and re-layouts  9.01 us (3%)
    pallas_call x1, Pallas kernels, gather(): pl.pallas_call(gather_kernel, out_shape=(jax.ShapeDtypeStruct((ROWS, COLS...  132 us
    pallas_call x1, Pallas kernels, compare(): pl.pallas_call(compare_kernel, out_shape=jax.ShapeDtypeStruct((COLS, PAY,...  62.5 us
    pallas_call x1, Pallas kernels, return_pay(): pl.pallas_call(return_kernel, out_shape=jax.ShapeDtypeStruct(pay.shape, p...  60.7 us
    pallas_call x1, Pallas kernels, finish(): pl.pallas_call(finish_kernel, out_shape=(jax.ShapeDtypeStruct((SLOTS, FRA...  9.42 us
    unnamed x13, local copies, waits for them, and re-layouts  8.41 us

profile of v1, /device:TPU:1, one launch (start us, length us, event | category | flops | bytes accessed | tf_op | source)
XLA Modules:
  0.0 276.6 jit_solution(10642853907675067195)
XLA Ops:
  0.6 0.0 copy-start.3
  0.6 0.0 copy-start.2
  0.7 0.0 copy-start.4
  0.7 6.2 %copy.14.feat = f32[16,4,9,1920]{3,2,1,0:T(8,128)} copy(f32[16,4,9,1920]{3,1,2,0:T(4,128)} %param.9) | data formatting | bytes 8847360 | tf_op args[0]
  6.9 0.0 copy-done.3
  6.9 0.0 copy-done.2
  6.9 0.0 copy-done.4
  6.9 0.6 broadcast_in_dim.2.idx
  7.5 131.7 %shard_map.104 = (bf16[8,16,576,128]{3,2,1,0:T(8,128)(2,1)}, s32[16,8,128]{2,1,0:T(8,128)}) custom-call(f32[16,4,9,1920]{3,2,1,0:T(8,128)} %copy.14.feat, s32[8,128]{1,0:T(8,128)} %broadcast_in_dim.2.idx), custom_call_target="tpu_custom_call" | custom-call | tf_op jit(solution)/shard_map/pallas_call | solution.py:205
  139.2 62.5 %shard_map.105.pay = bf16[16,880,128]{2,1,0:T(8,128)(2,1)} custom-call(s32[16,8,128]{2,1,0:T(8,128)} %get-tuple-element.6.idx, bf16[8,16,576,128]{3,2,1,0:T(8,128)(2,1)} %get-tuple-element.7.table), custom_call_target="tpu_custom_call" | custom-call | tf_op jit(solution)/shard_map/pallas_call | solution.py:320
  201.7 0.0 copy-start
  201.7 0.0 copy-start.1
  201.7 60.7 %shard_map.106.got = bf16[16,880,128]{2,1,0:T(8,128)(2,1)} custom-call(bf16[16,880,128]{2,1,0:T(8,128)(2,1)} %shard_map.105.pay), custom_call_target="tpu_custom_call" | custom-call | tf_op jit(solution)/shard_map/pallas_call | solution.py:395
  262.4 0.0 copy-done
  262.4 0.7 copy.15.second
  263.1 0.0 copy-done.1
  263.1 0.6 reduce
  264.4 9.4 %shard_map.107 = (f32[64,16]{1,0:T(8,128)}, f32[64,1]{1,0:T(8,128)}) custom-call(s32[1]{0:T(128)S(6)} %copy.17.count, bf16[16,880,128]{2,1,0:T(8,128)(2,1)} %shard_map.106.got, bf16[9,32]{1,0:T(8,128)(2,1)} %first.1, bf16[288,64]{1,0:T(8,128)(2,1)} %copy.15.second, bf16[576,128]{1,0:T(8,128)(2,1)} %third.1, bf16[9,128]{1,0:T(8,128)(2,1)} %bitcast.3), custom_call_target="tpu_custom_call" | custom-call | tf_op jit(solution)/shard_map/pallas_call | solution.py:526
  273.8 1.4 copy.16
  275.2 1.4 reduce.1
  (2 shorter events, 0.0 us)
Async XLA Ops:
  0.6 6.3 %copy-start.3 = (s32[64]{0:T(128)S(1)}, s32[64]{0:T(128)}, u32[]{:S(2)}) copy-start(s32[64]{0:T(128)} %param.10) | copy-start | bytes 772
  0.6 6.3 %copy-start.2 = (s32[64,1]{0,1:T(1,128)S(1)}, s32[64,1]{0,1:T(1,128)}, u32[]{:S(2)}) copy-start(s32[64,1]{0,1:T(1,128)} %param.11) | copy-start | bytes 772
  0.7 6.2 %copy-start.4 = (s32[64]{0:T(128)S(1)}, s32[64]{0:T(128)}, u32[]{:S(2)}) copy-start(s32[64]{0:T(128)} %param.12) | copy-start | bytes 772
  201.7 60.7 %copy-start = (bf16[288,64]{0,1:T(8,128)(2,1)S(1)}, bf16[288,64]{0,1:T(8,128)(2,1)}, u32[]{:S(2)}) copy-start(bf16[288,64]{0,1:T(8,128)(2,1)} %param.15) | copy-start | bytes 110596
  201.7 61.5 %copy-start.1 = (bf16[1152,1]{0,1:T(2,128)(2,1)S(1)}, bf16[1152,1]{0,1:T(2,128)(2,1)}, u32[]{:S(2)}) copy-start(bf16[1152,1]{0,1:T(2,128)(2,1)} %param.17) | copy-start | bytes 6916

commit v2 on v0

v2 whole, which is shorter than its diff:
```python
import functools

import jax
import jax.numpy as jnp
from jax import lax
from jax.experimental import pallas as pl
from jax.experimental.pallas import tpu as pltpu
from jax.sharding import PartitionSpec as P

MESH = pl.DeviceIdType.MESH
CLIPS = 16
FRAMES = 4
REGIONS = 9
DIM = 1920
LANES = 128
SLICES = DIM // LANES
COLS = 16
ROWS = 8
MAIN = 32
TILES = CLIPS + CLIPS * FRAMES // MAIN
SLOTS = 64
HALVES = 22
GROUPS = HALVES // 2
GROUP_ROWS = 2 * 40
PAY = GROUPS * GROUP_ROWS
VMEM_LIMIT = 60 * 2**20


def split(x):
    high = x.astype(jnp.bfloat16)
    return high, (x - high.astype(jnp.float32)).astype(jnp.bfloat16)


def dot_split(x, kernel):
    high, low = split(x)
    return jnp.dot(high, kernel, preferred_element_type=jnp.float32) + jnp.dot(
        low, kernel, preferred_element_type=jnp.float32
    )


def around(i, j):
    return [
        (dy * 3 + dx, (i + dy - 1) * 4 + j + dx - 1)
        for dy in range(3)
        for dx in range(3)
        if 0 <= i + dy - 1 < 4 and 0 <= j + dx - 1 < 4
    ]


def shift(x, by):
    return pltpu.roll(x, (LANES - by) % LANES, 1)


def make_units(feat, scales, end_scales):
    def measure():
        def quad(j, carry):
            ends = []
            for k in range(4):
                c = j * 4 + k
                parts = []
                for r in range(REGIONS):
                    x = feat[c, r]
                    total = jnp.sum(x * x, axis=-1, keepdims=True)
                    parts.append(jnp.broadcast_to(1.0 / jnp.sqrt(total + 1e-06), (FRAMES, LANES)))
                scales[c] = jnp.concatenate(parts[:8], axis=0)
                ends.append(parts[8])
            end_scales[j] = jnp.concatenate(ends, axis=0)
            return carry

        lax.fori_loop(0, CLIPS // 4, quad, 0)

    def fill(block, n):
        lanes = pl.ds(pl.multiple_of(n * LANES, LANES), LANES)

        def quad(j, carry):
            ends = []
            for k in range(4):
                c = j * 4 + k
                parts = [feat[c, r, :, lanes] for r in range(REGIONS)]
                main = jnp.concatenate(parts[:8], axis=0) * scales[c]
                block[c] = main.astype(jnp.bfloat16)
                ends.append(parts[8])
            end = jnp.concatenate(ends, axis=0) * end_scales[j]
            place = pl.ds(pl.multiple_of(lax.rem(j, 2) * 16, 16), 16)
            block[CLIPS + j // 2, place, :] = end.astype(jnp.bfloat16)
            return carry

        lax.fori_loop(0, CLIPS // 4, quad, 0)

    return measure, fill


def compare_owner(n, row, words, table, tails, pay):
    sub = lax.broadcasted_iota(jnp.int32, (8, LANES), 0)
    lane = lax.broadcasted_iota(jnp.int32, (8, LANES), 1)
    choice = jnp.where(lane < 96, lane // MAIN, (lane - 96) // FRAMES)

    def pick(parts):
        return jnp.where(choice == 0, parts[0], jnp.where(choice == 1, parts[1], parts[2]))

    def operand(main, ends):
        end = jnp.concatenate([jnp.where(sub < 4, ends[0], pltpu.roll(ends[1], 4, 0)), ends[2]], axis=0)
        return main + [end.astype(jnp.bfloat16)]

    def half(h):
        query_main, query_ends, target_main, target_ends = [], [], [], []
        for t in range(3):
            slot = jnp.minimum(t * HALVES + h, SLOTS - 1)
            query = words[n, 0, slot]
            query_main.append(table[(row * COLS + n) * TILES + query])
            query_ends.append(tails[(row * COLS + n) * CLIPS + query])
            target_main.append(table[words[n, 1, slot]])
            target_ends.append(tails[words[n, 2, slot]])
        right = operand(target_main, target_ends) + [jnp.zeros((16, LANES), jnp.bfloat16)]
        product = lax.dot_general(
            jnp.concatenate(operand(query_main, query_ends), axis=0),
            jnp.concatenate(right, axis=0),
            (((1,), (1,)), ((), ())),
            preferred_element_type=jnp.float32,
        )
        main = [
            pick([product[t * MAIN + k * 8 : t * MAIN + k * 8 + 8] for t in range(3)])
            for k in range(4)
        ]
        front = product[96:104]
        end = pick([front, pltpu.roll(front, 4, 0), product[104:112]])
        return jnp.concatenate(main, axis=0).astype(jnp.bfloat16), end

    def group(g, carry):
        base = pl.multiple_of(g * GROUP_ROWS, 16)
        ends = []
        for b in range(2):
            main, end = half(g * 2 + b)
            pay[n, pl.ds(base + b * MAIN, MAIN), :] = main
            ends.append(end)
        pay[n, pl.ds(base + 2 * MAIN, 16), :] = jnp.concatenate(ends, axis=0).astype(jnp.bfloat16)
        return carry

    lax.fori_loop(0, GROUPS, group, 0)


def chamfer(got, frames):
    lane = lax.broadcasted_iota(jnp.int32, (8, LANES), 1)
    frames[...] = jnp.zeros_like(frames)

    def best(x):
        top = jnp.maximum(x, shift(x, 4))
        top = jnp.maximum(top, shift(top, 8))
        top = jnp.maximum(top, shift(top, 16))
        ends = [shift(x, 96 + t * FRAMES - 32 * t) for t in range(3)]
        end = jnp.where(lane < 32, ends[0], jnp.where(lane < 64, ends[1], ends[2]))
        return jnp.maximum(top, end)

    def group(g, carry):
        base = pl.multiple_of(g * GROUP_ROWS, 16)
        total = got[0, pl.ds(base, GROUP_ROWS), :].astype(jnp.float32)
        for m in range(1, SLICES):
            total += got[m, pl.ds(base, GROUP_ROWS), :].astype(jnp.float32)
        for b in range(2):
            main = [best(total[b * MAIN + k * 8 : b * MAIN + k * 8 + 8]) for k in range(4)]
            main = (main[0] + main[1]) + (main[2] + main[3])
            end = best(total[2 * MAIN + b * 8 : 2 * MAIN + b * 8 + 8])
            value = (main + pltpu.roll(main, 4, 0) + end) * (1.0 / REGIONS)
            for f in range(FRAMES):
                frames[f, pl.ds(g * 2 + b, 1), :] = value[f : f + 1]
        return carry

    lax.fori_loop(0, GROUPS, group, 0)


def convolve(padded, kernels):
    channels = padded.shape[3]
    rows = padded.shape[2]
    total = None
    for dy in range(3):
        wide = jnp.concatenate(
            [padded[dy : dy + 4, dx : dx + 4] for dx in range(3)], axis=-1
        ).reshape(16 * rows, 3 * channels)
        part = dot_split(wide, kernels[dy])
        total = part if total is None else total + part
    return total


def refine(frames, first, second, third, last, maps, scores, one, two):
    pairs = 72
    one[...] = jnp.zeros_like(one)
    two[...] = jnp.zeros_like(two)
    ch1 = first.shape[1]
    ch2 = second.shape[0]
    ch3 = third.shape[1]
    taps = first[...].astype(jnp.float32)
    spread = []
    for i in range(FRAMES):
        value = frames[i]
        for j in range(FRAMES):
            spread.append(
                jnp.concatenate(
                    [
                        jnp.broadcast_to(value[:, 32 * t + j : 32 * t + j + 1], (24, ch1))
                        for t in range(3)
                    ],
                    axis=0,
                )
            )
    for i in range(FRAMES):
        for j in range(FRAMES):
            total = jnp.zeros((pairs, ch1), jnp.float32)
            for tap, pos in around(i, j):
                total += spread[pos] * taps[tap : tap + 1, :]
            one[1 + i, 1 + j] = jnp.maximum(total, 0.0)
    seconds = second[...].astype(jnp.float32).T.astype(jnp.bfloat16)
    hidden = convolve(one, [seconds[dy * 3 * ch1 : (dy + 1) * 3 * ch1] for dy in range(3)])
    two[1:5, 1:5] = jnp.maximum(hidden, 0.0).reshape(4, 4, pairs, ch2)
    hidden = convolve(two, [third[dy * 3 * ch2 : (dy + 1) * 3 * ch2, :] for dy in range(3)])
    high, low = split(jnp.maximum(hidden, 0.0))
    lasts = last[...].astype(jnp.float32)
    lasts = jnp.concatenate(
        [lasts[:, tap * ch3 : (tap + 1) * ch3] for tap in range(9)]
        + [jnp.zeros((7, ch3), jnp.float32)],
        axis=0,
    ).astype(jnp.bfloat16)
    nt = (((1,), (1,)), ((), ()))
    response = lax.dot_general(high, lasts, nt, preferred_element_type=jnp.float32)
    response += lax.dot_general(low, lasts, nt, preferred_element_type=jnp.float32)
    response = response.reshape(16, pairs, response.shape[1])
    tap_lane = lax.broadcasted_iota(jnp.int32, (pairs, response.shape[2]), 1)
    out_lane = lax.broadcasted_iota(jnp.int32, (pairs, LANES), 1)
    result = jnp.zeros((pairs, LANES), jnp.float32)
    for i in range(FRAMES):
        for j in range(FRAMES):
            total = jnp.zeros((pairs, response.shape[2]), jnp.float32)
            for tap, pos in around(i, j):
                total += jnp.where(tap_lane == tap, response[pos], 0.0)
            value = jnp.sum(total, axis=1, keepdims=True)
            result = jnp.where(out_lane == i * 4 + j, value, result)
    result = jnp.clip(result, -1.0, 1.0)
    top = jnp.maximum(result, shift(result, 1))
    top = jnp.maximum(top, shift(top, 2))
    kept = (out_lane < 16) & (lax.rem(out_lane, 4) == 0)
    score = jnp.sum(jnp.where(kept, top, 0.0), axis=1, keepdims=True) * (1.0 / FRAMES)
    result = jnp.where(out_lane == 16, score, result)
    result = jnp.concatenate([result, jnp.zeros((LANES - pairs, LANES), jnp.float32)], axis=0).T
    for t in range(3):
        amount = min(HALVES, SLOTS - t * HALVES)
        place = slice(t * HALVES, t * HALVES + amount)
        maps[:, place] = result[:16, t * 24 : t * 24 + amount]
        scores[:, place] = result[16:17, t * 24 : t * 24 + amount]


def kernel(
    idx,
    feat,
    first,
    second,
    third,
    last,
    maps,
    scores,
    table,
    idx_all,
    words,
    units,
    scales,
    end_scales,
    tails,
    pay,
    got,
    frames,
    one,
    two,
    a_send,
    a_recv,
    i_send,
    i_recv,
    b_send,
    b_recv,
    p_send,
    p_recv,
    own_sem,
):
    row = lax.axis_index("row")
    me = lax.axis_index("col")
    z = row // 2
    core = lax.rem(row, 2)
    my_y = me // 4
    my_x = lax.rem(me, 4)
    rows_z = lambda step: lax.rem(z + step, 4) * 2 + core
    rows_mate = lambda step: lax.rem(z + step, 4) * 2 + 1 - core
    mate = z * 2 + 1 - core
    offset = lambda i: lax.rem(7 * i, COLS)
    to = lambda i: lax.rem(my_y + offset(i) // 4, 4) * 4 + lax.rem(my_x + lax.rem(offset(i), 4), 4)
    source = lambda i: (
        lax.rem(my_y + 4 - offset(i) // 4, 4) * 4 + lax.rem(my_x + 4 - lax.rem(offset(i), 4), 4)
    )
    blocks = lambda r, c: table.at[pl.ds((r * COLS + c) * TILES, TILES)]
    measure, fill = make_units(feat, scales, end_scales)

    def loop(start, stop, body):
        def step(i, carry):
            body(i)
            return carry

        lax.fori_loop(start, stop, step, 0)

    barrier = pltpu.get_barrier_semaphore()

    def greet(device_row, device_col):
        pl.semaphore_signal(
            barrier, inc=1, device_id=(device_row, device_col), device_id_type=MESH
        )

    loop(1, COLS, lambda i: greet(row, to(i)))
    for other in (rows_z(1), rows_z(2), rows_z(3), mate):
        greet(other, me)

    def plane_copy(src, dst, send, recv, i, n):
        return pltpu.make_async_remote_copy(
            src_ref=src,
            dst_ref=dst,
            send_sem=send.at[i],
            recv_sem=recv.at[i],
            device_id=(row, n),
            device_id_type=MESH,
        )

    idx_copy = lambda i: plane_copy(idx, idx_all.at[me], i_send, i_recv, i, to(i))
    slice_copy = lambda i: plane_copy(units.at[to(i)], blocks(row, me), a_send, a_recv, i, to(i))
    slice_arrival = lambda i: plane_copy(
        units.at[0], blocks(row, source(i)), a_send, a_recv, i, to(i)
    )
    part_copy = lambda i: plane_copy(pay.at[to(i)], got.at[me], p_send, p_recv, i, to(i))
    part_arrival = lambda i: plane_copy(pay.at[0], got.at[source(i)], p_send, p_recv, i, to(i))

    def forward(source_row, s, target_row, kind, i):
        return pltpu.make_async_remote_copy(
            src_ref=blocks(source_row, s),
            dst_ref=blocks(source_row, s),
            send_sem=b_send.at[kind, i],
            recv_sem=b_recv.at[kind, i],
            device_id=(target_row, me),
            device_id_type=MESH,
        )

    def spread(i):
        s = source(i)
        for step in (1, 3, 2):
            forward(row, s, rows_z(step), step, i).start()
        forward(row, s, mate, 4, i).start()

    measure()
    pl.semaphore_wait(barrier, COLS - 1 + 4)

    @pl.when(me < SLICES)
    def _():
        fill(blocks(row, me), me)
        spread(0)

    idx_all[me] = idx[...]
    loop(1, COLS, lambda i: idx_copy(i).start())

    def send_slice(i):
        n = to(i)

        @pl.when(n < SLICES)
        def _():
            fill(units.at[n], n)
            slice_copy(i).start()

    loop(1, COLS, send_slice)

    @pl.when(me < SLICES)
    def _():
        def pass_on(i):
            slice_arrival(i).wait_recv()
            spread(i)

        loop(1, COLS, pass_on)

        def relay(i):
            s = source(i)
            for step in (1, 3, 2):
                block_row = rows_z(4 - step)
                forward(block_row, s, rows_z(step), step, i).wait_recv()
                forward(block_row, s, mate, 4 + step, i).start()

        loop(0, COLS, relay)

        def settle(i):
            s = source(i)
            forward(rows_mate(0), s, mate, 4, i).wait_recv()
            for step in (1, 3, 2):
                forward(rows_mate(4 - step), s, mate, 4 + step, i).wait_recv()

        loop(0, COLS, settle)

    loop(1, COLS, lambda i: idx_copy(i).wait())

    @pl.when(me < SLICES)
    def _():
        local = pltpu.make_async_copy(idx_all, words, own_sem.at[0])
        local.start()

        def widen(i):
            for k in range(2):
                ends = table[i * TILES + CLIPS + k].astype(jnp.float32)
                for p in range(4):
                    pair = ends[p * 8 : p * 8 + 8]
                    tails[i * CLIPS + k * 8 + p * 2] = pair
                    tails[i * CLIPS + k * 8 + p * 2 + 1] = pltpu.roll(pair, 4, 0)

        loop(0, ROWS * COLS, widen)
        local.wait()

        def send_part(i):
            compare_owner(to(i), row, words, table, tails, pay)
            part_copy(i).start()

        loop(1, COLS, send_part)
        compare_owner(me, row, words, table, tails, pay)
        mine = pltpu.make_async_copy(pay.at[me], got.at[me], own_sem.at[1])
        mine.start()
        mine.wait()

    def take_part(i):
        @pl.when(source(i) < SLICES)
        def _():
            part_arrival(i).wait_recv()

    loop(1, COLS, take_part)
    chamfer(got, frames)
    refine(frames, first, second, third, last, maps, scores, one, two)

    def drain_slice(i):
        @pl.when(to(i) < SLICES)
        def _():
            slice_copy(i).wait_send()

    loop(1, COLS, drain_slice)

    @pl.when(me < SLICES)
    def _():
        loop(1, COLS, lambda i: part_copy(i).wait_send())

        def drain(i):
            s = source(i)
            forward(row, s, mate, 4, i).wait_send()
            for step in (1, 3, 2):
                forward(row, s, rows_z(step), step, i).wait_send()
                forward(rows_z(4 - step), s, mate, 4 + step, i).wait_send()

        loop(0, COLS, drain)


def per_device(
    features,
    query_row,
    target_device,
    target_row,
    pair_count,
    conv_first,
    conv_second,
    conv_third,
    conv_last,
):
    device = target_device[:, 0]
    asked = jnp.stack([query_row, device * TILES + target_row, device * CLIPS + target_row])
    asked = jnp.pad(asked, ((0, 5), (0, LANES - SLOTS)))
    vmem = pl.BlockSpec(memory_space=pltpu.VMEM)
    dma = pltpu.SemaphoreType.DMA
    bf16, f32, i32 = jnp.bfloat16, jnp.float32, jnp.int32
    maps, scores = pl.pallas_call(
        kernel,
        out_shape=(
            jax.ShapeDtypeStruct((FRAMES * FRAMES, SLOTS), f32),
            jax.ShapeDtypeStruct((1, SLOTS), f32),
        ),
        in_specs=[vmem] * 6,
        out_specs=[vmem] * 2,
        scratch_shapes=[
            pltpu.VMEM((ROWS * COLS * TILES, MAIN, LANES), bf16),
            pltpu.VMEM((COLS, 8, LANES), i32),
            pltpu.SMEM((COLS, 8, LANES), i32),
            pltpu.VMEM((SLICES, TILES, MAIN, LANES), bf16),
            pltpu.VMEM((CLIPS, MAIN, LANES), f32),
            pltpu.VMEM((CLIPS // 4, 16, LANES), f32),
            pltpu.VMEM((ROWS * COLS * CLIPS, 8, LANES), f32),
            pltpu.VMEM((COLS, PAY, LANES), bf16),
            pltpu.VMEM((COLS, PAY, LANES), bf16),
            pltpu.VMEM((FRAMES, 24, LANES), f32),
            pltpu.VMEM((6, 6, 72, conv_first.shape[1]), f32),
            pltpu.VMEM((6, 6, 72, conv_second.shape[1]), f32),
            dma((COLS,)),
            dma((COLS,)),
            dma((COLS,)),
            dma((COLS,)),
            dma((8, COLS)),
            dma((8, COLS)),
            dma((COLS,)),
            dma((COLS,)),
            dma((2,)),
        ],
        compiler_params=pltpu.CompilerParams(
            collective_id=0, has_side_effects=True, vmem_limit_bytes=VMEM_LIMIT
        ),
    )(
        asked,
        features.transpose(0, 2, 1, 3),
        conv_first,
        conv_second.T,
        conv_third,
        conv_last.T,
    )
    live = lax.broadcasted_iota(jnp.int32, (1, SLOTS), 1) < pair_count[0]
    return jnp.where(live, maps, 0.0).T, jnp.where(live, scores, 0.0)[0]


def solution(mesh):
    return jax.shard_map(
        per_device,
        mesh=mesh,
        in_specs=(
            P(("row", "col"), None, None, None),
            P(("row", "col")),
            P(("row", "col"), None),
            P(("row", "col")),
            P(("row", "col")),
            P(),
            P(),
            P(),
            P(),
        ),
        out_specs=(P(("row", "col"), None), P(("row", "col"))),
        check_vma=False,
    )
```

time: 593 us -> 183 us (0.31)
  waiting for transfers between devices: 285 us -> 0 us
  Pallas kernels: 0 us -> 176 us
  local copies, waits for them, and re-layouts: 155 us -> 0.6 us
  matrix products: 66.8 us -> 0 us
  starting transfers between devices: 52.4 us -> 0 us
  other arithmetic: 28.7 us -> 3.79 us
    all_to_all x3 -> x0, waiting for transfers between devices: 285 us -> none  [the longest x1 276 us: move_blocks(): lax.all_to_all(blocks, ('row', 'col'), split_axis=0, concat_axis=0, tiled...]
    pallas_call x0 -> x1, Pallas kernels: none -> 176 us  [per_device(): pl.pallas_call(kernel, out_shape=(jax.ShapeDtypeStruct((FRAMES * FRAMES,...]
    gather x18 -> x0, local copies, waits for them, and re-layouts: 98.9 us -> none  [the longest x16 92 us: compute_group(): return compare_pairs(left_table[left_ids], right_table[right_ids], kernels)]
    dot_general x104 -> x0, matrix products: 66.8 us -> none  [the longest x96 46.7 us: convolve(): jnp.einsum('bijc,co->bijo', wide[:, shift:shift + frames], parts[shift],...]
    all_to_all x3 -> x0, starting transfers between devices: 52.4 us -> none  [the longest x1 30.8 us: per_device(): lax.all_to_all(refined, ('row', 'col'), split_axis=0, concat_axis=0, tile...]
    scatter x2 -> x0, local copies, waits for them, and re-layouts: 24.7 us -> none  [the longest x1 23.9 us: per_device(): jnp.zeros((buffer_slots,) + table.shape[1:], jnp.bfloat16).at[slot_index]]
    while x40 -> x0, local copies, waits for them, and re-layouts: 12.2 us -> none
    select_n x13 -> x0, other arithmetic: 10.7 us -> none  [the longest x1 8.49 us: per_device(): jnp.where(is_live[:, None, None], table[query_row], jnp.zeros((), jnp.bfl...]
  transfers between devices with their start and end apart: 3 -> 0, of which waited for: 2 -> 0; matrix products, arithmetic and copies ran while one was open for 10% -> 0% of each run, Pallas kernels for 0% -> 0%
where the time goes in v2:
time: 183 us; the launch traced here: 182 us
  Pallas kernels  176 us (96%)
  other arithmetic  3.79 us (2%)
    pallas_call x1, Pallas kernels, per_device(): pl.pallas_call(kernel, out_shape=(jax.ShapeDtypeStruct((FRAMES * FRAMES,...  176 us

profile of v2, /device:TPU:1, one launch (start us, length us, event | category | flops | bytes accessed | tf_op | source)
XLA Modules:
  0.0 181.6 jit_solution(6361401349084168127)
XLA Ops:
  1.3 0.7 fusion.2
  2.0 0.7 pad_add_fusion
  2.6 0.6 pad.4.idx
  3.2 175.9 %shard_map.104 = (f32[16,64]{1,0:T(8,128)}, f32[1,64]{1,0:T(1,128)}) custom-call(s32[8,128]{1,0:T(8,128)} %pad.4.idx, f32[16,9,4,1920]{3,2,1,0:T(4,128)} %bitcast.23, bf16[9,32]{1,0:T(8,128)(2,1)} %first.1, bf16[64,288]{1,0:T(8,128)(2,1)} %bitcast.24, bf16[576,128]{1,0:T(8,128)(2,1)} %third.1, bf16[1,1152]{1,0:T(2,128)(2,1)} %bitcast.25), custom_call_target="tpu_custom_call" | custom-call | tf_op jit(solution)/shard_map/pallas_call | solution.py:471
  179.1 1.3 select_bitcast_fusion
  180.4 1.1 fusion
  (1 shorter events, 0.0 us)

commit v3 on v2

--- a/solution.py
+++ b/solution.py
@@ -21,8 +21,8 @@
 SLOTS = 64
 HALVES = 22
 GROUPS = HALVES // 2
-GROUP_ROWS = 2 * 40
-PAY = GROUPS * GROUP_ROWS
+ENDS = HALVES * MAIN
+PAY = ENDS + 96
 VMEM_LIMIT = 60 * 2**20
 
 
@@ -126,17 +126,19 @@
         end = pick([front, pltpu.roll(front, 4, 0), product[104:112]])
         return jnp.concatenate(main, axis=0).astype(jnp.bfloat16), end
 
-    def group(g, carry):
-        base = pl.multiple_of(g * GROUP_ROWS, 16)
+    sub_low = sub < 4
+    rows = []
+    for g in range(GROUPS):
         ends = []
         for b in range(2):
-            main, end = half(g * 2 + b)
-            pay[n, pl.ds(base + b * MAIN, MAIN), :] = main
+            h = g * 2 + b
+            pay[n, h * MAIN : (h + 1) * MAIN, :], end = half(h)
             ends.append(end)
-        pay[n, pl.ds(base + 2 * MAIN, 16), :] = jnp.concatenate(ends, axis=0).astype(jnp.bfloat16)
-        return carry
-
-    lax.fori_loop(0, GROUPS, group, 0)
+        rows.append(jnp.where(sub_low, ends[0], pltpu.roll(ends[1], 4, 0)))
+    rows.append(rows[-1])
+    for k in range(len(rows) // 2):
+        pair = jnp.concatenate(rows[2 * k : 2 * k + 2], axis=0)
+        pay[n, ENDS + k * 16 : ENDS + k * 16 + 16, :] = pair.astype(jnp.bfloat16)
 
 
 def chamfer(got, frames):
@@ -151,21 +153,29 @@
         end = jnp.where(lane < 32, ends[0], jnp.where(lane < 64, ends[1], ends[2]))
         return jnp.maximum(top, end)
 
-    def group(g, carry):
-        base = pl.multiple_of(g * GROUP_ROWS, 16)
-        total = got[0, pl.ds(base, GROUP_ROWS), :].astype(jnp.float32)
+    def add(start, amount):
+        total = got[0, pl.ds(start, amount), :].astype(jnp.float32)
         for m in range(1, SLICES):
-            total += got[m, pl.ds(base, GROUP_ROWS), :].astype(jnp.float32)
-        for b in range(2):
-            main = [best(total[b * MAIN + k * 8 : b * MAIN + k * 8 + 8]) for k in range(4)]
+            total += got[m, pl.ds(start, amount), :].astype(jnp.float32)
+        return total
+
+    def quad(g, carry):
+        base = pl.multiple_of(g * 4 * MAIN, MAIN)
+        ends = add(pl.multiple_of(ENDS + g * 16, 16), 16)
+        for b in range(4):
+            total = add(pl.multiple_of(base + b * MAIN, MAIN), MAIN)
+            main = [best(total[k * 8 : k * 8 + 8]) for k in range(4)]
             main = (main[0] + main[1]) + (main[2] + main[3])
-            end = best(total[2 * MAIN + b * 8 : 2 * MAIN + b * 8 + 8])
-            value = (main + pltpu.roll(main, 4, 0) + end) * (1.0 / REGIONS)
+            main = main + pltpu.roll(main, 4, 0)
+            end = best(ends[b // 2 * 8 : b // 2 * 8 + 8])
+            if b % 2:
+                end = pltpu.roll(end, 4, 0)
+            value = (main + end) * (1.0 / REGIONS)
             for f in range(FRAMES):
-                frames[f, pl.ds(g * 2 + b, 1), :] = value[f : f + 1]
+                frames[f, pl.ds(g * 4 + b, 1), :] = value[f : f + 1]
         return carry
 
-    lax.fori_loop(0, GROUPS, group, 0)
+    lax.fori_loop(0, 24 // 4, quad, 0)
 
 
 def convolve(padded, kernels):
@@ -248,7 +258,9 @@
 
 
 def kernel(
-    idx,
+    query_row,
+    target_device,
+    target_row,
     feat,
     first,
     second,
@@ -257,6 +269,7 @@
     maps,
     scores,
     table,
+    idx,
     idx_all,
     words,
     units,
@@ -343,7 +356,7 @@
 
     def spread(i):
         s = source(i)
-        for step in (1, 3, 2):
+        for step in (1, 3):
             forward(row, s, rows_z(step), step, i).start()
         forward(row, s, mate, 4, i).start()
 
@@ -355,6 +368,10 @@
         fill(blocks(row, me), me)
         spread(0)
 
+    idx[...] = jnp.zeros_like(idx)
+    idx[0:1, :SLOTS] = query_row[...]
+    idx[1:2, :SLOTS] = target_device[...] * TILES + target_row[...]
+    idx[2:3, :SLOTS] = target_device[...] * CLIPS + target_row[...]
     idx_all[me] = idx[...]
     loop(1, COLS, lambda i: idx_copy(i).start())
 
@@ -378,12 +395,24 @@
 
         def relay(i):
             s = source(i)
-            for step in (1, 3, 2):
+            for step in (1, 3):
                 block_row = rows_z(4 - step)
                 forward(block_row, s, rows_z(step), step, i).wait_recv()
+
+                @pl.when(lax.rem(i, 2) == step // 2)
+                def _():
+                    forward(block_row, s, rows_z(step), 2, i).start()
+
                 forward(block_row, s, mate, 4 + step, i).start()
 
         loop(0, COLS, relay)
+
+        def relay_far(i):
+            s = source(i)
+            forward(rows_z(2), s, rows_z(1), 2, i).wait_recv()
+            forward(rows_z(2), s, mate, 6, i).start()
+
+        loop(0, COLS, relay_far)
 
         def settle(i):
             s = source(i)
@@ -413,10 +442,12 @@
 
         def send_part(i):
             compare_owner(to(i), row, words, table, tails, pay)
-            part_copy(i).start()
-
-        loop(1, COLS, send_part)
-        compare_owner(me, row, words, table, tails, pay)
+
+            @pl.when(i < COLS)
+            def _():
+                part_copy(i).start()
+
+        loop(1, COLS + 1, send_part)
         mine = pltpu.make_async_copy(pay.at[me], got.at[me], own_sem.at[1])
         mine.start()
         mine.wait()
@@ -444,9 +475,16 @@
         def drain(i):
             s = source(i)
             forward(row, s, mate, 4, i).wait_send()
-            for step in (1, 3, 2):
+            for step in (1, 3):
+                block_row = rows_z(4 - step)
                 forward(row, s, rows_z(step), step, i).wait_send()
-                forward(rows_z(4 - step), s, mate, 4 + step, i).wait_send()
+                forward(block_row, s, mate, 4 + step, i).wait_send()
+
+                @pl.when(lax.rem(i, 2) == step // 2)
+                def _():
+                    forward(block_row, s, rows_z(step), 2, i).wait_send()
+
+            forward(rows_z(2), s, mate, 6, i).wait_send()
 
         loop(0, COLS, drain)
 
@@ -462,9 +500,6 @@
     conv_third,
     conv_last,
 ):
-    device = target_device[:, 0]
-    asked = jnp.stack([query_row, device * TILES + target_row, device * CLIPS + target_row])
-    asked = jnp.pad(asked, ((0, 5), (0, LANES - SLOTS)))
     vmem = pl.BlockSpec(memory_space=pltpu.VMEM)
     dma = pltpu.SemaphoreType.DMA
     bf16, f32, i32 = jnp.bfloat16, jnp.float32, jnp.int32
@@ -474,10 +509,11 @@
             jax.ShapeDtypeStruct((FRAMES * FRAMES, SLOTS), f32),
             jax.ShapeDtypeStruct((1, SLOTS), f32),
         ),
-        in_specs=[vmem] * 6,
+        in_specs=[vmem] * 8,
         out_specs=[vmem] * 2,
         scratch_shapes=[
             pltpu.VMEM((ROWS * COLS * TILES, MAIN, LANES), bf16),
+            pltpu.VMEM((8, LANES), i32),
             pltpu.VMEM((COLS, 8, LANES), i32),
             pltpu.SMEM((COLS, 8, LANES), i32),
             pltpu.VMEM((SLICES, TILES, MAIN, LANES), bf16),
@@ -503,7 +539,9 @@
             collective_id=0, has_side_effects=True, vmem_limit_bytes=VMEM_LIMIT
         ),
     )(
-        asked,
+        query_row.reshape(1, SLOTS),
+        target_device.reshape(1, SLOTS),
+        target_row.reshape(1, SLOTS),
         features.transpose(0, 2, 1, 3),
         conv_first,
         conv_second.T,

time: 183 us -> 155 us (0.85)
  the two profiles are of different devices: /device:TPU:1 before, /device:TPU:5 now
where the time goes in v3:
time: 155 us; the launch traced here: 154 us
  Pallas kernels  151 us (97%)
  other arithmetic  2.48 us (2%)
    pallas_call x1, Pallas kernels, per_device(): pl.pallas_call(kernel, out_shape=(jax.ShapeDtypeStruct((FRAMES * FRAMES,...  151 us

profile of v3, /device:TPU:5, one launch (start us, length us, event | category | flops | bytes accessed | tf_op | source)
XLA Modules:
  0.0 154.5 jit_solution(15989527226538635911)
XLA Ops:
  1.3 150.7 %shard_map.104 = (f32[16,64]{1,0:T(8,128)}, f32[1,64]{1,0:T(1,128)}) custom-call(s32[1,64]{1,0:T(1,128)} %bitcast.16, s32[1,64]{1,0:T(1,128)} %bitcast.17, s32[1,64]{1,0:T(1,128)} %bitcast.18, f32[16,9,4,1920]{3,2,1,0:T(4,128)} %bitcast.13, bf16[9,32]{1,0:T(8,128)(2,1)} %first.1, bf16[64,288]{1,0:T(8,128)(2,1)} %bitcast.14, bf16[576,128]{1,0:T(8,128)(2,1)} %third.1, ...), custom_call_target="tpu_custom_call" | custom-call | tf_op jit(solution)/shard_map/pallas_call | solution.py:506
  152.0 1.3 select_bitcast_fusion
  153.3 1.2 fusion
  (1 shorter events, 0.0 us)

commit v4 on v3

--- a/solution.py
+++ b/solution.py
@@ -20,9 +20,12 @@
 TILES = CLIPS + CLIPS * FRAMES // MAIN
 SLOTS = 64
 HALVES = 22
-GROUPS = HALVES // 2
-ENDS = HALVES * MAIN
-PAY = ENDS + 96
+PAIRS = 72
+QUAD = 4 * MAIN + 16
+STAGES = ((0, 0, 8), (4, 8, 4), (8, 12, 4), (14, 16, 4), (16, 20, 2))
+STARTS = tuple(first // 4 * QUAD for _, first, _ in STAGES)
+SIZES = tuple(amount * MAIN + -(-amount // 4) * 16 for _, _, amount in STAGES)
+PAY = STARTS[-1] + SIZES[-1]
 VMEM_LIMIT = 60 * 2**20
 
 
@@ -90,7 +93,50 @@
     return measure, fill
 
 
-def compare_owner(n, row, words, table, tails, pay):
+def sort_kernel(count, query_row, target_device, target_row, idx, place):
+    z = lax.axis_index("row") // 2
+    a = lax.broadcasted_iota(jnp.int32, (LANES, LANES), 0)
+    b = lax.broadcasted_iota(jnp.int32, (LANES, LANES), 1)
+
+    def lines(x):
+        wide = jnp.concatenate([x, jnp.zeros((1, LANES - SLOTS), jnp.int32)], axis=1)
+        wide = jnp.broadcast_to(wide.astype(jnp.float32), (LANES, LANES))
+        return wide, wide.T
+
+    device = target_device[...]
+    far = (device >> 5) == lax.rem(z + 2, 4)
+    key_b, key_a = lines(jnp.where(far, 1 + (device & 15), 0))
+    earlier = (a < SLOTS) & ((key_a < key_b) | ((key_a == key_b) & (a < b)))
+    rank_b = jnp.sum(earlier.astype(jnp.float32), axis=0, keepdims=True)
+    earlier = (b < SLOTS) & ((key_b < key_a) | ((key_b == key_a) & (b < a)))
+    rank_a = jnp.sum(earlier.astype(jnp.float32), axis=1, keepdims=True)
+    taken = (rank_a == b.astype(jnp.float32)) & (a < SLOTS)
+
+    def ordered(x):
+        kept = jnp.where(taken, lines(x)[1], 0.0)
+        return jnp.sum(kept, axis=0, keepdims=True).astype(jnp.int32)
+
+    rows = [ordered(query_row[...]), ordered(device * CLIPS + target_row[...])]
+    idx[...] = jnp.concatenate(rows + [jnp.zeros((6, LANES), jnp.int32)], axis=0)
+    position = (3 * lax.rem(a, 24) + a // 24).astype(jnp.float32)
+    match = (position == rank_b) & (a < PAIRS) & (b < SLOTS) & (b < count[0])
+    place[...] = jnp.where(match, 1.0, 0.0).astype(jnp.bfloat16)
+
+
+def sort_slots(count, query_row, target_device, target_row):
+    vmem = pl.BlockSpec(memory_space=pltpu.VMEM)
+    return pl.pallas_call(
+        sort_kernel,
+        out_shape=(
+            jax.ShapeDtypeStruct((8, LANES), jnp.int32),
+            jax.ShapeDtypeStruct((LANES, LANES), jnp.bfloat16),
+        ),
+        in_specs=[pl.BlockSpec(memory_space=pltpu.SMEM)] + [vmem] * 3,
+        out_specs=[vmem] * 2,
+    )(count, query_row, target_device, target_row)
+
+
+def compare_owner(n, stage, row, words, mains, tails, pay):
     sub = lax.broadcasted_iota(jnp.int32, (8, LANES), 0)
     lane = lax.broadcasted_iota(jnp.int32, (8, LANES), 1)
     choice = jnp.where(lane < 96, lane // MAIN, (lane - 96) // FRAMES)
@@ -105,12 +151,13 @@
     def half(h):
         query_main, query_ends, target_main, target_ends = [], [], [], []
         for t in range(3):
-            slot = jnp.minimum(t * HALVES + h, SLOTS - 1)
+            slot = min(3 * h + t, SLOTS - 1)
             query = words[n, 0, slot]
-            query_main.append(table[(row * COLS + n) * TILES + query])
+            target = words[n, 1, slot]
+            query_main.append(mains[(row * COLS + n) * CLIPS + query])
             query_ends.append(tails[(row * COLS + n) * CLIPS + query])
-            target_main.append(table[words[n, 1, slot]])
-            target_ends.append(tails[words[n, 2, slot]])
+            target_main.append(mains[target])
+            target_ends.append(tails[target])
         right = operand(target_main, target_ends) + [jnp.zeros((16, LANES), jnp.bfloat16)]
         product = lax.dot_general(
             jnp.concatenate(operand(query_main, query_ends), axis=0),
@@ -126,24 +173,23 @@
         end = pick([front, pltpu.roll(front, 4, 0), product[104:112]])
         return jnp.concatenate(main, axis=0).astype(jnp.bfloat16), end
 
-    sub_low = sub < 4
-    rows = []
-    for g in range(GROUPS):
-        ends = []
-        for b in range(2):
-            h = g * 2 + b
-            pay[n, h * MAIN : (h + 1) * MAIN, :], end = half(h)
-            ends.append(end)
-        rows.append(jnp.where(sub_low, ends[0], pltpu.roll(ends[1], 4, 0)))
-    rows.append(rows[-1])
-    for k in range(len(rows) // 2):
-        pair = jnp.concatenate(rows[2 * k : 2 * k + 2], axis=0)
-        pay[n, ENDS + k * 16 : ENDS + k * 16 + 16, :] = pair.astype(jnp.bfloat16)
-
-
-def chamfer(got, frames):
+    _, first, amount = STAGES[stage]
+    for base in range(0, amount, 4):
+        start = STARTS[stage] + base // 4 * QUAD
+        several = min(4, amount - base)
+        rows = []
+        for b in range(0, several, 2):
+            ends = []
+            for k in (b, b + 1):
+                pay[n, start + k * MAIN : start + (k + 1) * MAIN, :], end = half(first + base + k)
+                ends.append(end)
+            rows.append(jnp.where(sub < 4, ends[0], pltpu.roll(ends[1], 4, 0)))
+        rows = jnp.concatenate([rows[0], rows[-1]], axis=0).astype(jnp.bfloat16)
+        pay[n, start + several * MAIN : start + several * MAIN + 16, :] = rows
+
+
+def chamfer(got, frames, first, stop):
     lane = lax.broadcasted_iota(jnp.int32, (8, LANES), 1)
-    frames[...] = jnp.zeros_like(frames)
 
     def best(x):
         top = jnp.maximum(x, shift(x, 4))
@@ -159,11 +205,11 @@
             total += got[m, pl.ds(start, amount), :].astype(jnp.float32)
         return total
 
-    def quad(g, carry):
-        base = pl.multiple_of(g * 4 * MAIN, MAIN)
-        ends = add(pl.multiple_of(ENDS + g * 16, 16), 16)
-        for b in range(4):
-            total = add(pl.multiple_of(base + b * MAIN, MAIN), MAIN)
+    def quad(q, amount):
+        base = pl.multiple_of(q * QUAD, 16)
+        ends = add(pl.multiple_of(base + amount * MAIN, 16), 16)
+        for b in range(amount):
+            total = add(pl.multiple_of(base + b * MAIN, 16), MAIN)
             main = [best(total[k * 8 : k * 8 + 8]) for k in range(4)]
             main = (main[0] + main[1]) + (main[2] + main[3])
             main = main + pltpu.roll(main, 4, 0)
@@ -172,10 +218,17 @@
                 end = pltpu.roll(end, 4, 0)
             value = (main + end) * (1.0 / REGIONS)
             for f in range(FRAMES):
-                frames[f, pl.ds(g * 4 + b, 1), :] = value[f : f + 1]
-        return carry
-
-    lax.fori_loop(0, 24 // 4, quad, 0)
+                frames[f, pl.ds(q * 4 + b, 1), :] = value[f : f + 1]
+
+    if (stop - first) % 4:
+        quad(first // 4, stop - first)
+    else:
+
+        def step(q, carry):
+            quad(q, 4)
+            return carry
+
+        lax.fori_loop(first // 4, stop // 4, step, 0)
 
 
 def convolve(padded, kernels):
@@ -191,8 +244,8 @@
     return total
 
 
-def refine(frames, first, second, third, last, maps, scores, one, two):
-    pairs = 72
+def refine(frames, place, first, second, third, last, maps, scores, one, two):
+    pairs = PAIRS
     one[...] = jnp.zeros_like(one)
     two[...] = jnp.zeros_like(two)
     ch1 = first.shape[1]
@@ -250,17 +303,20 @@
     score = jnp.sum(jnp.where(kept, top, 0.0), axis=1, keepdims=True) * (1.0 / FRAMES)
     result = jnp.where(out_lane == 16, score, result)
     result = jnp.concatenate([result, jnp.zeros((LANES - pairs, LANES), jnp.float32)], axis=0).T
-    for t in range(3):
-        amount = min(HALVES, SLOTS - t * HALVES)
-        place = slice(t * HALVES, t * HALVES + amount)
-        maps[:, place] = result[:16, t * 24 : t * 24 + amount]
-        scores[:, place] = result[16:17, t * 24 : t * 24 + amount]
+    result = result[:24]
+    high, low = split(result)
+    rest = result - high.astype(jnp.float32) - low.astype(jnp.float32)
+    result = sum(
+        jnp.dot(part, place[...], preferred_element_type=jnp.float32)
+        for part in (rest.astype(jnp.bfloat16), low, high)
+    )
+    maps[...] = result[:16, :SLOTS]
+    scores[...] = result[16:17, :SLOTS]
 
 
 def kernel(
-    query_row,
-    target_device,
-    target_row,
+    idx,
+    place,
     feat,
     first,
     second,
@@ -269,12 +325,12 @@
     maps,
     scores,
     table,
-    idx,
     idx_all,
     words,
     units,
     scales,
     end_scales,
+    mains,
     tails,
     pay,
     got,
@@ -341,15 +397,41 @@
     slice_arrival = lambda i: plane_copy(
         units.at[0], blocks(row, source(i)), a_send, a_recv, i, to(i)
     )
-    part_copy = lambda i: plane_copy(pay.at[to(i)], got.at[me], p_send, p_recv, i, to(i))
-    part_arrival = lambda i: plane_copy(pay.at[0], got.at[source(i)], p_send, p_recv, i, to(i))
-
-    def forward(source_row, s, target_row, kind, i):
+
+    def part(buffer, n, stage):
+        return buffer.at[n, pl.ds(STARTS[stage], SIZES[stage])]
+
+    def part_copy(i, stage):
+        return plane_copy(
+            part(pay, to(i), stage),
+            part(got, me, stage),
+            p_send.at[stage],
+            p_recv.at[stage],
+            i,
+            to(i),
+        )
+
+    def part_arrival(i, stage):
+        return plane_copy(
+            part(pay, 0, stage),
+            part(got, source(i), stage),
+            p_send.at[stage],
+            p_recv.at[stage],
+            i,
+            to(i),
+        )
+
+    def own_part(stage):
+        return pltpu.make_async_copy(
+            part(pay, me, stage), part(got, me, stage), own_sem.at[1 + stage]
+        )
+
+    def forward(source_row, s, target_row, kind):
         return pltpu.make_async_remote_copy(
             src_ref=blocks(source_row, s),
             dst_ref=blocks(source_row, s),
-            send_sem=b_send.at[kind, i],
-            recv_sem=b_recv.at[kind, i],
+            send_sem=b_send.at[kind, s],
+            recv_sem=b_recv.at[kind, s],
             device_id=(target_row, me),
             device_id_type=MESH,
         )
@@ -357,8 +439,8 @@
     def spread(i):
         s = source(i)
         for step in (1, 3):
-            forward(row, s, rows_z(step), step, i).start()
-        forward(row, s, mate, 4, i).start()
+            forward(row, s, rows_z(step), step).start()
+        forward(row, s, mate, 4).start()
 
     measure()
     pl.semaphore_wait(barrier, COLS - 1 + 4)
@@ -368,10 +450,6 @@
         fill(blocks(row, me), me)
         spread(0)
 
-    idx[...] = jnp.zeros_like(idx)
-    idx[0:1, :SLOTS] = query_row[...]
-    idx[1:2, :SLOTS] = target_device[...] * TILES + target_row[...]
-    idx[2:3, :SLOTS] = target_device[...] * CLIPS + target_row[...]
     idx_all[me] = idx[...]
     loop(1, COLS, lambda i: idx_copy(i).start())
 
@@ -393,32 +471,23 @@
 
         loop(1, COLS, pass_on)
 
-        def relay(i):
-            s = source(i)
+        def relay(s):
             for step in (1, 3):
                 block_row = rows_z(4 - step)
-                forward(block_row, s, rows_z(step), step, i).wait_recv()
-
-                @pl.when(lax.rem(i, 2) == step // 2)
+                forward(block_row, s, rows_z(step), step).wait_recv()
+
+                @pl.when(lax.rem(s, 2) == step // 2)
                 def _():
-                    forward(block_row, s, rows_z(step), 2, i).start()
-
-                forward(block_row, s, mate, 4 + step, i).start()
+                    forward(block_row, s, rows_z(step), 2).start()
+
+                forward(block_row, s, mate, 4 + step).start()
 
         loop(0, COLS, relay)
 
-        def relay_far(i):
-            s = source(i)
-            forward(rows_z(2), s, rows_z(1), 2, i).wait_recv()
-            forward(rows_z(2), s, mate, 6, i).start()
-
-        loop(0, COLS, relay_far)
-
-        def settle(i):
-            s = source(i)
-            forward(rows_mate(0), s, mate, 4, i).wait_recv()
-            for step in (1, 3, 2):
-                forward(rows_mate(4 - step), s, mate, 4 + step, i).wait_recv()
+        def settle(s):
+            forward(rows_mate(0), s, mate, 4).wait_recv()
+            forward(rows_mate(3), s, mate, 5).wait_recv()
+            forward(rows_mate(1), s, mate, 7).wait_recv()
 
         loop(0, COLS, settle)
 
@@ -429,7 +498,10 @@
         local = pltpu.make_async_copy(idx_all, words, own_sem.at[0])
         local.start()
 
-        def widen(i):
+        def settle_block(block_row, s):
+            i = block_row * COLS + s
+            for c in range(CLIPS):
+                mains[i * CLIPS + c] = table[i * TILES + c]
             for k in range(2):
                 ends = table[i * TILES + CLIPS + k].astype(jnp.float32)
                 for p in range(4):
@@ -437,29 +509,56 @@
                     tails[i * CLIPS + k * 8 + p * 2] = pair
                     tails[i * CLIPS + k * 8 + p * 2 + 1] = pltpu.roll(pair, 4, 0)
 
-        loop(0, ROWS * COLS, widen)
+        def settle_near(k):
+            step = k // 32
+            block_row = lax.rem(z + step + step // 2, 4) * 2 + lax.rem(k // COLS, 2)
+            settle_block(block_row, lax.rem(k, COLS))
+
+        loop(0, 6 * COLS, settle_near)
         local.wait()
-
-        def send_part(i):
-            compare_owner(to(i), row, words, table, tails, pay)
-
-            @pl.when(i < COLS)
+        begin = 0
+        for stage, (stop, _, _) in enumerate(STAGES):
+
+            def relay_far(s):
+                forward(rows_z(2), s, rows_z(1), 2).wait_recv()
+                forward(rows_z(2), s, mate, 6).start()
+
+            def settle_far(s):
+                forward(rows_mate(2), s, mate, 6).wait_recv()
+                settle_block(rows_z(2), s)
+                settle_block(rows_mate(2), s)
+
+            if stop > begin:
+                loop(begin, stop, relay_far)
+                loop(begin, stop, settle_far)
+            begin = stop
+
+            def send_part(i, stage=stage):
+                compare_owner(to(i), stage, row, words, mains, tails, pay)
+
+                @pl.when(i < COLS)
+                def _():
+                    part_copy(i, stage).start()
+
+            loop(1, COLS + 1, send_part)
+            own_part(stage).start()
+
+    frames[...] = jnp.zeros_like(frames)
+    for stage, (_, first_group, amount) in enumerate(STAGES):
+
+        def take_part(i, stage=stage):
+            @pl.when(source(i) < SLICES)
             def _():
-                part_copy(i).start()
-
-        loop(1, COLS + 1, send_part)
-        mine = pltpu.make_async_copy(pay.at[me], got.at[me], own_sem.at[1])
-        mine.start()
-        mine.wait()
-
-    def take_part(i):
-        @pl.when(source(i) < SLICES)
-        def _():
-            part_arrival(i).wait_recv()
-
-    loop(1, COLS, take_part)
-    chamfer(got, frames)
-    refine(frames, first, second, third, last, maps, scores, one, two)
+                part_arrival(i, stage).wait_recv()
+
+        loop(1, COLS, take_part)
+
+        @pl.when(me < SLICES)
+        def _(stage=stage):
+            own_part(stage).wait()
+
+        chamfer(got, frames, first_group, first_group + amount)
+    refine(frames, place, first, second, third, last, maps, scores, one, two)
 
     def drain_slice(i):
         @pl.when(to(i) < SLICES)
@@ -470,21 +569,21 @@
 
     @pl.when(me < SLICES)
     def _():
-        loop(1, COLS, lambda i: part_copy(i).wait_send())
-
-        def drain(i):
-            s = source(i)
-            forward(row, s, mate, 4, i).wait_send()
+        for stage in range(len(STAGES)):
+            loop(1, COLS, lambda i, stage=stage: part_copy(i, stage).wait_send())
+
+        def drain(s):
+            forward(row, s, mate, 4).wait_send()
             for step in (1, 3):
                 block_row = rows_z(4 - step)
-                forward(row, s, rows_z(step), step, i).wait_send()
-                forward(block_row, s, mate, 4 + step, i).wait_send()
-
-                @pl.when(lax.rem(i, 2) == step // 2)
+                forward(row, s, rows_z(step), step).wait_send()
+                forward(block_row, s, mate, 4 + step).wait_send()
+
+                @pl.when(lax.rem(s, 2) == step // 2)
                 def _():
-                    forward(block_row, s, rows_z(step), 2, i).wait_send()
-
-            forward(rows_z(2), s, mate, 6, i).wait_send()
+                    forward(block_row, s, rows_z(step), 2).wait_send()
+
+            forward(rows_z(2), s, mate, 6).wait_send()
 
         loop(0, COLS, drain)
 
@@ -500,6 +599,12 @@
     conv_third,
     conv_last,
 ):
+    idx, place = sort_slots(
+        pair_count,
+        query_row.reshape(1, SLOTS),
+        target_device.reshape(1, SLOTS),
+        target_row.reshape(1, SLOTS),
+    )
     vmem = pl.BlockSpec(memory_space=pltpu.VMEM)
     dma = pltpu.SemaphoreType.DMA
     bf16, f32, i32 = jnp.bfloat16, jnp.float32, jnp.int32
@@ -509,16 +614,16 @@
             jax.ShapeDtypeStruct((FRAMES * FRAMES, SLOTS), f32),
             jax.ShapeDtypeStruct((1, SLOTS), f32),
         ),
-        in_specs=[vmem] * 8,
+        in_specs=[vmem] * 7,
         out_specs=[vmem] * 2,
         scratch_shapes=[
             pltpu.VMEM((ROWS * COLS * TILES, MAIN, LANES), bf16),
-            pltpu.VMEM((8, LANES), i32),
             pltpu.VMEM((COLS, 8, LANES), i32),
             pltpu.SMEM((COLS, 8, LANES), i32),
             pltpu.VMEM((SLICES, TILES, MAIN, LANES), bf16),
             pltpu.VMEM((CLIPS, MAIN, LANES), f32),
             pltpu.VMEM((CLIPS // 4, 16, LANES), f32),
+            pltpu.VMEM((ROWS * COLS * CLIPS, MAIN, LANES), bf16),
             pltpu.VMEM((ROWS * COLS * CLIPS, 8, LANES), f32),
             pltpu.VMEM((COLS, PAY, LANES), bf16),
             pltpu.VMEM((COLS, PAY, LANES), bf16),
@@ -531,25 +636,23 @@
             dma((COLS,)),
             dma((8, COLS)),
             dma((8, COLS)),
-            dma((COLS,)),
-            dma((COLS,)),
-            dma((2,)),
+            dma((len(STAGES), COLS)),
+            dma((len(STAGES), COLS)),
+            dma((1 + len(STAGES),)),
         ],
         compiler_params=pltpu.CompilerParams(
             collective_id=0, has_side_effects=True, vmem_limit_bytes=VMEM_LIMIT
         ),
     )(
-        query_row.reshape(1, SLOTS),
-        target_device.reshape(1, SLOTS),
-        target_row.reshape(1, SLOTS),
+        idx,
+        place,
         features.transpose(0, 2, 1, 3),
         conv_first,
         conv_second.T,
         conv_third,
         conv_last.T,
     )
-    live = lax.broadcasted_iota(jnp.int32, (1, SLOTS), 1) < pair_count[0]
-    return jnp.where(live, maps, 0.0).T, jnp.where(live, scores, 0.0)[0]
+    return maps.T, scores[0]
 
 
 def solution(mesh):

time: 155 us -> 132 us (0.85)
  the two profiles are of different devices: /device:TPU:5 before, /device:TPU:1 now
where the time goes in v4:
time: 132 us; the launch traced here: 131 us
  Pallas kernels  128 us (97%)
  local copies, waits for them, and re-layouts  2.41 us (2%)
    pallas_call x1, Pallas kernels, per_device(): pl.pallas_call(kernel, out_shape=(jax.ShapeDtypeStruct((FRAMES * FRAMES,...  126 us

profile of v4, /device:TPU:1, one launch (start us, length us, event | category | flops | bytes accessed | tf_op | source)
XLA Modules:
  0.0 131.2 jit_solution(13472242736903403629)
XLA Ops:
  1.3 1.5 %shard_map.104 = (s32[8,128]{1,0:T(8,128)}, bf16[128,128]{1,0:T(8,128)(2,1)}) custom-call(s32[1]{0:T(128)S(6)} %copy.13.count, s32[1,64]{1,0:T(1,128)} %bitcast.12, s32[1,64]{1,0:T(1,128)} %bitcast.13, s32[1,64]{1,0:T(1,128)} %bitcast.14), custom_call_target="tpu_custom_call" | custom-call | tf_op jit(solution)/shard_map/pallas_call | solution.py:128
  2.8 126.0 %shard_map.105 = (f32[16,64]{1,0:T(8,128)}, f32[1,64]{1,0:T(1,128)}) custom-call(s32[8,128]{1,0:T(8,128)} %get-tuple-element.6.idx, bf16[128,128]{1,0:T(8,128)(2,1)} %get-tuple-element.7.place, f32[16,9,4,1920]{3,2,1,0:T(4,128)} %bitcast.8, bf16[9,32]{1,0:T(8,128)(2,1)} %first.1, bf16[64,288]{1,0:T(8,128)(2,1)} %bitcast.9, bf16[576,128]{1,0:T(8,128)(2,1)} %third.1, ...), custom_call_target="tpu_custom_call" | custom-call | tf_op jit(solution)/shard_map/pallas_call | solution.py:611
  128.8 1.3 copy.14
  130.1 1.1 copy.15

commit v5 on v4

--- a/solution.py
+++ b/solution.py
@@ -26,7 +26,8 @@
 STARTS = tuple(first // 4 * QUAD for _, first, _ in STAGES)
 SIZES = tuple(amount * MAIN + -(-amount // 4) * 16 for _, _, amount in STAGES)
 PAY = STARTS[-1] + SIZES[-1]
-VMEM_LIMIT = 60 * 2**20
+AHEAD = 4
+VMEM_LIMIT = 62 * 2**20
 
 
 def split(x):
@@ -54,12 +55,13 @@
     return pltpu.roll(x, (LANES - by) % LANES, 1)
 
 
-def make_units(feat, scales, end_scales):
+def make_units(load, feat, scales, end_scales):
     def measure():
         def quad(j, carry):
             ends = []
             for k in range(4):
                 c = j * 4 + k
+                load(c).wait()
                 parts = []
                 for r in range(REGIONS):
                     x = feat[c, r]
@@ -244,13 +246,10 @@
     return total
 
 
-def refine(frames, place, first, second, third, last, maps, scores, one, two):
+def refine(frames, place, first, seconds, third, lasts, maps, scores, one, two):
     pairs = PAIRS
-    one[...] = jnp.zeros_like(one)
-    two[...] = jnp.zeros_like(two)
     ch1 = first.shape[1]
-    ch2 = second.shape[0]
-    ch3 = third.shape[1]
+    ch2 = seconds.shape[1]
     taps = first[...].astype(jnp.float32)
     spread = []
     for i in range(FRAMES):
@@ -271,20 +270,13 @@
             for tap, pos in around(i, j):
                 total += spread[pos] * taps[tap : tap + 1, :]
             one[1 + i, 1 + j] = jnp.maximum(total, 0.0)
-    seconds = second[...].astype(jnp.float32).T.astype(jnp.bfloat16)
-    hidden = convolve(one, [seconds[dy * 3 * ch1 : (dy + 1) * 3 * ch1] for dy in range(3)])
+    hidden = convolve(one, [seconds[dy * 3 * ch1 : (dy + 1) * 3 * ch1, :] for dy in range(3)])
     two[1:5, 1:5] = jnp.maximum(hidden, 0.0).reshape(4, 4, pairs, ch2)
     hidden = convolve(two, [third[dy * 3 * ch2 : (dy + 1) * 3 * ch2, :] for dy in range(3)])
     high, low = split(jnp.maximum(hidden, 0.0))
-    lasts = last[...].astype(jnp.float32)
-    lasts = jnp.concatenate(
-        [lasts[:, tap * ch3 : (tap + 1) * ch3] for tap in range(9)]
-        + [jnp.zeros((7, ch3), jnp.float32)],
-        axis=0,
-    ).astype(jnp.bfloat16)
     nt = (((1,), (1,)), ((), ()))
-    response = lax.dot_general(high, lasts, nt, preferred_element_type=jnp.float32)
-    response += lax.dot_general(low, lasts, nt, preferred_element_type=jnp.float32)
+    response = lax.dot_general(high, lasts[...], nt, preferred_element_type=jnp.float32)
+    response += lax.dot_general(low, lasts[...], nt, preferred_element_type=jnp.float32)
     response = response.reshape(16, pairs, response.shape[1])
     tap_lane = lax.broadcasted_iota(jnp.int32, (pairs, response.shape[2]), 1)
     out_lane = lax.broadcasted_iota(jnp.int32, (pairs, LANES), 1)
@@ -317,13 +309,14 @@
 def kernel(
     idx,
     place,
-    feat,
+    features,
     first,
     second,
     third,
     last,
     maps,
     scores,
+    feat,
     table,
     idx_all,
     words,
@@ -337,6 +330,8 @@
     frames,
     one,
     two,
+    seconds,
+    lasts,
     a_send,
     a_recv,
     i_send,
@@ -346,6 +341,7 @@
     p_send,
     p_recv,
     own_sem,
+    feat_sem,
 ):
     row = lax.axis_index("row")
     me = lax.axis_index("col")
@@ -362,7 +358,8 @@
         lax.rem(my_y + 4 - offset(i) // 4, 4) * 4 + lax.rem(my_x + 4 - lax.rem(offset(i), 4), 4)
     )
     blocks = lambda r, c: table.at[pl.ds((r * COLS + c) * TILES, TILES)]
-    measure, fill = make_units(feat, scales, end_scales)
+    load = lambda c: pltpu.make_async_copy(features.at[c], feat.at[c], feat_sem.at[c])
+    measure, fill = make_units(load, feat, scales, end_scales)
 
     def loop(start, stop, body):
         def step(i, carry):
@@ -371,6 +368,7 @@
 
         lax.fori_loop(start, stop, step, 0)
 
+    loop(0, CLIPS, lambda c: load(c).start())
     barrier = pltpu.get_barrier_semaphore()
 
     def greet(device_row, device_col):
@@ -442,6 +440,16 @@
             forward(row, s, rows_z(step), step).start()
         forward(row, s, mate, 4).start()
 
+    frames[...] = jnp.zeros_like(frames)
+    one[...] = jnp.zeros_like(one)
+    two[...] = jnp.zeros_like(two)
+    seconds[...] = second[...].astype(jnp.float32).T.astype(jnp.bfloat16)
+    ch3 = third.shape[1]
+    lasts[...] = jnp.concatenate(
+        [last[:, tap * ch3 : (tap + 1) * ch3].astype(jnp.float32) for tap in range(9)]
+        + [jnp.zeros((7, ch3), jnp.float32)],
+        axis=0,
+    ).astype(jnp.bfloat16)
     measure()
     pl.semaphore_wait(barrier, COLS - 1 + 4)
 
@@ -461,15 +469,22 @@
             fill(units.at[n], n)
             slice_copy(i).start()
 
-    loop(1, COLS, send_slice)
+    def pass_on(i):
+        @pl.when(me < SLICES)
+        def _():
+            slice_arrival(i).wait_recv()
+            spread(i)
+
+    def send_and_pass(i):
+        send_slice(i)
+        pass_on(i - AHEAD)
+
+    loop(1, AHEAD + 1, send_slice)
+    loop(AHEAD + 1, COLS, send_and_pass)
+    loop(COLS - AHEAD, COLS, pass_on)
 
     @pl.when(me < SLICES)
     def _():
-        def pass_on(i):
-            slice_arrival(i).wait_recv()
-            spread(i)
-
-        loop(1, COLS, pass_on)
 
         def relay(s):
             for step in (1, 3):
@@ -517,7 +532,7 @@
         loop(0, 6 * COLS, settle_near)
         local.wait()
         begin = 0
-        for stage, (stop, _, _) in enumerate(STAGES):
+        for stage, (stop, _, amount) in enumerate(STAGES):
 
             def relay_far(s):
                 forward(rows_z(2), s, rows_z(1), 2).wait_recv()
@@ -533,17 +548,21 @@
                 loop(begin, stop, settle_far)
             begin = stop
 
-            def send_part(i, stage=stage):
-                compare_owner(to(i), stage, row, words, mains, tails, pay)
-
-                @pl.when(i < COLS)
-                def _():
-                    part_copy(i, stage).start()
-
-            loop(1, COLS + 1, send_part)
+            several = max(1, 8 // amount)
+
+            def send_parts(step, stage=stage, several=several):
+                some = [1 + step * several + k for k in range(several)]
+                for i in some:
+                    compare_owner(to(i), stage, row, words, mains, tails, pay)
+                for i in some:
+
+                    @pl.when(i < COLS)
+                    def _(i=i):
+                        part_copy(i, stage).start()
+
+            loop(0, COLS // several, send_parts)
             own_part(stage).start()
 
-    frames[...] = jnp.zeros_like(frames)
     for stage, (_, first_group, amount) in enumerate(STAGES):
 
         def take_part(i, stage=stage):
@@ -558,7 +577,7 @@
             own_part(stage).wait()
 
         chamfer(got, frames, first_group, first_group + amount)
-    refine(frames, place, first, second, third, last, maps, scores, one, two)
+    refine(frames, place, first, seconds, third, lasts, maps, scores, one, two)
 
     def drain_slice(i):
         @pl.when(to(i) < SLICES)
@@ -614,9 +633,10 @@
             jax.ShapeDtypeStruct((FRAMES * FRAMES, SLOTS), f32),
             jax.ShapeDtypeStruct((1, SLOTS), f32),
         ),
-        in_specs=[vmem] * 7,
+        in_specs=[vmem] * 2 + [pl.BlockSpec(memory_space=pl.ANY)] + [vmem] * 4,
         out_specs=[vmem] * 2,
         scratch_shapes=[
+            pltpu.VMEM((CLIPS, REGIONS, FRAMES, DIM), f32),
             pltpu.VMEM((ROWS * COLS * TILES, MAIN, LANES), bf16),
             pltpu.VMEM((COLS, 8, LANES), i32),
             pltpu.SMEM((COLS, 8, LANES), i32),
@@ -630,6 +650,8 @@
             pltpu.VMEM((FRAMES, 24, LANES), f32),
             pltpu.VMEM((6, 6, 72, conv_first.shape[1]), f32),
             pltpu.VMEM((6, 6, 72, conv_second.shape[1]), f32),
+            pltpu.VMEM(conv_second.shape, bf16),
+            pltpu.VMEM((16, conv_third.shape[1]), bf16),
             dma((COLS,)),
             dma((COLS,)),
             dma((COLS,)),
@@ -639,6 +661,7 @@
             dma((len(STAGES), COLS)),
             dma((len(STAGES), COLS)),
             dma((1 + len(STAGES),)),
+            dma((CLIPS,)),
         ],
         compiler_params=pltpu.CompilerParams(
             collective_id=0, has_side_effects=True, vmem_limit_bytes=VMEM_LIMIT

time: 132 us -> 131 us (level)
  no operation moved by 1% of the time
where the time goes in v5:
time: 131 us
  Pallas kernels  127 us (97%)
  local copies, waits for them, and re-layouts  2.41 us (2%)
    pallas_call x1, Pallas kernels, per_device(): pl.pallas_call(kernel, out_shape=(jax.ShapeDtypeStruct((FRAMES * FRAMES,...  126 us

profile of v5, /device:TPU:1, one launch (start us, length us, event | category | flops | bytes accessed | tf_op | source)
XLA Modules:
  0.0 130.8 jit_solution(16831459128972824933)
XLA Ops:
  1.3 1.5 %shard_map.104 = (s32[8,128]{1,0:T(8,128)}, bf16[128,128]{1,0:T(8,128)(2,1)}) custom-call(s32[1]{0:T(128)S(6)} %copy.13.count, s32[1,64]{1,0:T(1,128)} %bitcast.12, s32[1,64]{1,0:T(1,128)} %bitcast.13, s32[1,64]{1,0:T(1,128)} %bitcast.14), custom_call_target="tpu_custom_call" | custom-call | tf_op jit(solution)/shard_map/pallas_call | solution.py:130
  2.8 125.6 %shard_map.105 = (f32[16,64]{1,0:T(8,128)}, f32[1,64]{1,0:T(1,128)}) custom-call(s32[8,128]{1,0:T(8,128)} %get-tuple-element.6.idx, bf16[128,128]{1,0:T(8,128)(2,1)} %get-tuple-element.7.place, f32[16,9,4,1920]{3,2,1,0:T(4,128)} %bitcast.8, bf16[9,32]{1,0:T(8,128)(2,1)} %first.1, bf16[64,288]{1,0:T(8,128)(2,1)} %bitcast.9, bf16[576,128]{1,0:T(8,128)(2,1)} %third.1, ...), custom_call_target="tpu_custom_call" | custom-call | tf_op jit(solution)/shard_map/pallas_call | solution.py:630
  128.4 1.3 copy.14
  129.7 1.1 copy.15
